TPU v7x, 32 devices: a whole 2x2x4 slice. The times are simulated.
32 devices in a mesh: seq: 8 (over z, x), section: 2 (over core), dp: 2 (over y).
Axes of the slice: x: 2, y: 2, z: 4, core: 2. Of those that a mesh axis runs over, the one named last changes fastest.
Arguments:
- queries: bfloat16 [2, 1024, 3584], P('section', 'seq', 'dp'), may hold values from -5 to 5
- key_vectors: bfloat16 [2, 1024, 3584], P('section', 'seq', 'dp'), may hold values from -5 to 5
- value_vectors: bfloat16 [2, 1024, 3584], P('section', 'seq', 'dp'), may hold values from -6 to 6
- out_grad: bfloat16 [2, 1024, 3584], P('section', 'seq', 'dp'), may hold values from -6 to 6
- doc_lengths: int32 [8], replicated, may hold values from 1 to 384, 1024 in all
Outputs:
- query_grad: bfloat16 [2, 1024, 3584], P('section', 'seq', 'dp')
- key_grad: bfloat16 [2, 1024, 3584], P('section', 'seq', 'dp')
- value_grad: bfloat16 [2, 1024, 3584], P('section', 'seq', 'dp')
Inputs may be any that keep to these rules, and one draw needn't show every extreme that they name: `doc_lengths`: the 8 lengths sum to 1024; the longest is exactly 384.
All inputs are finite; a program needn't handle non-finite values.
Results may differ from a plain program's by a relative error of at most 0.024.
Values may be sent and summed in bfloat16 or wider, within the bound.
No kernel may reach another device: no remote copies, remote signals or barrier semaphores. Data moves between devices by JAX's collectives and lax.ppermute only.
A program may use at most 192 MiB of HBM per device.

v0:
```python
import functools
import math
import jax
import jax.numpy as jnp
from jax import lax
from jax.experimental import pallas as pl
from jax.experimental.pallas import tpu as pltpu
from jax.sharding import PartitionSpec as P

HEAD = 224
LANES = 128
FLOOR = -1e30


def pick_slot(stacked, slot):
    return lax.dynamic_index_in_dim(stacked, slot, 0, keepdims=False)


def put_slot(stacked, update, slot):
    return lax.dynamic_update_index_in_dim(stacked, update, slot, 0)


def spread_shards(queries, key_vectors, value_vectors, out_grad, doc_lengths):
    local_rows = queries.shape[1]
    local_width = queries.shape[2]
    head_count = local_width // HEAD
    seq_size = lax.axis_size("seq")
    group = seq_size // head_count
    scaling = HEAD ** (-0.5)

    def spread(matrix):
        shaped = matrix.reshape(local_rows, head_count, 1, HEAD)
        copies = jnp.broadcast_to(shaped, (local_rows, head_count, group, HEAD))
        return copies.reshape(local_rows, seq_size * HEAD)

    query_head, key_head, value_head, cot_head = (
        lax.all_to_all(spread(queries), "seq", split_axis=1, concat_axis=0, tiled=True),
        lax.all_to_all(spread(key_vectors), "seq", split_axis=1, concat_axis=0, tiled=True),
        lax.all_to_all(spread(value_vectors), "seq", split_axis=1, concat_axis=0, tiled=True),
        lax.all_to_all(spread(out_grad), "seq", split_axis=1, concat_axis=0, tiled=True),
    )
    length = key_head.shape[0]
    member = lax.axis_index("seq") % group
    blocks = 2 * group
    block = length // blocks
    bounds = jnp.cumsum(doc_lengths)
    positions = jnp.arange(length, dtype=jnp.int32)
    doc_index = jnp.sum((positions[:, None] >= bounds[None, :]).astype(jnp.int32), axis=1)
    row_list = [member, blocks - 1 - member]
    query_list = []
    cot_list = []
    pos_list = []
    for which in range(2):
        offset = row_list[which] * block
        query_list.append(lax.dynamic_slice_in_dim(query_head, offset, block, 0))
        cot_list.append(lax.dynamic_slice_in_dim(cot_head, offset, block, 0))
        pos_list.append(offset + jnp.arange(block, dtype=jnp.int32))
    query_stack = jnp.stack(query_list)
    cot_stack = jnp.stack(cot_list)
    pos_stack = jnp.stack(pos_list)
    doc_stack = jnp.take(doc_index, pos_stack)
    plan = []
    for number in range(blocks + 1):
        first = number <= member
        slot = jnp.where(first, 0, 1).astype(jnp.int32)
        col_block = jnp.where(first, number, number - member - 1)
        flag = None
        plan.append((slot, col_block, flag))
    row_max = jnp.full((2, block), -jnp.inf, jnp.float32)
    row_sum = jnp.zeros((2, block), jnp.float32)
    stored = []
    for slot, col_block, flag in plan:

        def score_tile(carry, slot=slot, col_block=col_block):
            maxima, totals = carry
            query_rows = pick_slot(query_stack, slot)
            key_rows = lax.dynamic_slice_in_dim(key_head, col_block * block, block, 0)
            col_docs = lax.dynamic_slice_in_dim(doc_index, col_block * block, block, 0)
            col_positions = col_block * block + jnp.arange(block, dtype=jnp.int32)
            raw = jnp.dot(query_rows, key_rows.T, preferred_element_type=jnp.float32) * scaling
            allowed = (pick_slot(doc_stack, slot)[:, None] == col_docs[None, :]) & (
                pick_slot(pos_stack, slot)[:, None] >= col_positions[None, :]
            )
            scores = jnp.where(allowed, raw, -jnp.inf)
            before = pick_slot(maxima, slot)
            after = jnp.maximum(before, jnp.max(scores, axis=1))
            safe = jnp.where(jnp.isfinite(after), after, 0.0)
            total = pick_slot(totals, slot) * jnp.exp(before - safe) + jnp.sum(
                jnp.exp(scores - safe[:, None]), axis=1
            )
            return (scores, put_slot(maxima, after, slot), put_slot(totals, total, slot))

        scores, row_max, row_sum = score_tile((row_max, row_sum))
        stored.append(scores)

    def tile_weights(scores, slot):
        return (
            jnp.exp(scores - pick_slot(row_max, slot)[:, None]) / pick_slot(row_sum, slot)[:, None]
        )

    summed = jnp.zeros((2, block, HEAD), jnp.float32)
    for (slot, col_block, flag), scores in zip(plan, stored):

        def add_values(carry, slot=slot, col_block=col_block, scores=scores):
            rounded = tile_weights(scores, slot).astype(jnp.bfloat16)
            value_rows = lax.dynamic_slice_in_dim(value_head, col_block * block, block, 0)
            term = jnp.dot(rounded, value_rows, preferred_element_type=jnp.float32)
            return put_slot(carry, pick_slot(carry, slot) + term, slot)

        summed = add_values(summed)
    attended = summed.astype(jnp.bfloat16)
    row_dot = jnp.sum(cot_stack.astype(jnp.float32) * attended.astype(jnp.float32), axis=2)
    query_acc = jnp.zeros((2, block, HEAD), jnp.float32)
    key_acc = jnp.zeros((length, HEAD), jnp.float32)
    value_acc = jnp.zeros((length, HEAD), jnp.float32)
    for (slot, col_block, flag), scores in zip(plan, stored):

        def backward_tile(carry, slot=slot, col_block=col_block, scores=scores):
            query_sum, key_sum, value_sum = carry
            weights = tile_weights(scores, slot)
            rounded = weights.astype(jnp.bfloat16)
            query_rows = pick_slot(query_stack, slot)
            cot_rows = pick_slot(cot_stack, slot)
            start = col_block * block
            key_rows = lax.dynamic_slice_in_dim(key_head, start, block, 0)
            value_rows = lax.dynamic_slice_in_dim(value_head, start, block, 0)
            value_term = jnp.dot(rounded.T, cot_rows, preferred_element_type=jnp.float32)
            prob_grad = jnp.dot(cot_rows, value_rows.T, preferred_element_type=jnp.float32)
            score_grad = (
                weights * (prob_grad - pick_slot(row_dot, slot)[:, None]) * scaling
            ).astype(jnp.bfloat16)
            query_term = jnp.dot(score_grad, key_rows, preferred_element_type=jnp.float32)
            key_term = jnp.dot(score_grad.T, query_rows, preferred_element_type=jnp.float32)
            query_sum = put_slot(query_sum, pick_slot(query_sum, slot) + query_term, slot)
            key_sum = lax.dynamic_update_slice_in_dim(
                key_sum, lax.dynamic_slice_in_dim(key_sum, start, block, 0) + key_term, start, 0
            )
            value_sum = lax.dynamic_update_slice_in_dim(
                value_sum,
                lax.dynamic_slice_in_dim(value_sum, start, block, 0) + value_term,
                start,
                0,
            )
            return (query_sum, key_sum, value_sum)

        query_acc, key_acc, value_acc = backward_tile((query_acc, key_acc, value_acc))
    query_rounded = query_acc.astype(jnp.bfloat16)
    key_back, value_back = (
        lax.all_to_all(key_acc, "seq", split_axis=0, concat_axis=1, tiled=True),
        lax.all_to_all(value_acc, "seq", split_axis=0, concat_axis=1, tiled=True),
    )

    def settle(received):
        shaped = received.astype(jnp.float32).reshape(local_rows, head_count, group, HEAD)
        return jnp.sum(shaped, axis=2).reshape(1, local_rows, local_width).astype(jnp.bfloat16)

    query_full = jnp.zeros((length, HEAD), jnp.bfloat16)
    for which in range(2):
        query_full = lax.dynamic_update_slice_in_dim(
            query_full, query_rounded[which], row_list[which] * block, 0
        )
    query_back = lax.all_to_all(query_full, "seq", split_axis=0, concat_axis=1, tiled=True)
    query_out = settle(query_back)
    return (query_out, settle(key_back), settle(value_back))


NT = ((1,), (1,))
NN = ((1,), (0,))
TN = ((0,), (0,))
GROUP = 8


def head_span(head):
    low = head * HEAD // LANES * LANES
    high = -(-(head + 1) * HEAD // LANES) * LANES
    return low, high


def head_mask(head):
    low, high = head_span(head)
    lane = lax.broadcasted_iota(jnp.int32, (1, high - low), 1) + low
    inside = (lane >= head * HEAD) & (lane < (head + 1) * HEAD)
    return inside.astype(jnp.float32).astype(jnp.bfloat16)


def matmul(left, right, dims):
    return lax.dot_general(left, right, (dims, ((), ())), preferred_element_type=jnp.float32)


def stack(values, axis):
    return values[0] if len(values) == 1 else jnp.concatenate(values, axis=axis)


def allowed(lengths_ref, rows, query_block, key_block):
    shape = (rows, rows)
    position = query_block * rows + lax.broadcasted_iota(jnp.int32, shape, 1)
    keys = key_block * rows + lax.broadcasted_iota(jnp.int32, shape, 0)
    start = jnp.zeros_like(position)
    bound = jnp.int32(0)
    for doc in range(lengths_ref.shape[0]):
        bound = bound + lengths_ref[doc]
        start = jnp.where(position >= bound, bound, start)
    return (keys >= start) & (keys <= position)


def make_tile(lengths_ref, rows, queries, keys):
    mask = stack(
        [stack([allowed(lengths_ref, rows, q, k) for _, q in queries], 1) for _, k in keys], 0
    )
    return [slot for slot, _ in queries], [slot for slot, _ in keys], mask


def tile_values(plan, head, queries, keys, products):
    low, high = head_span(head)
    keep = head_mask(head)

    def gather(refs, number, slots):
        return stack([refs[slot][number][0, :, low:high] for slot in slots], 0)

    out = []
    for query_slots, key_slots, _ in plan:
        q = [gather(queries, number, query_slots) for number in range(products)]
        k = [gather(keys, number, key_slots) * keep for number in range(products)]
        out.append((q, k, [matmul(b, a, NT) for a, b in zip(q, k)]))
    return out, keep


def tiles_ahead(heads, plan, queries, keys, products):
    ready = tile_values(plan, 0, queries, keys, products)
    for head in range(heads):
        now = ready
        if head + 1 < heads:
            ready = tile_values(plan, head + 1, queries, keys, products)
        yield head, now


def plans(third, lengths_ref, rows, me):
    def even():
        return [make_tile(lengths_ref, rows, ((0, me), (1, me + 1)), ((0, me), (1, me - 2)))]

    def odd(extra=()):
        met = ((0, me), (1, me - 1)) + extra
        return [
            make_tile(lengths_ref, rows, ((0, me),), ((0, me),)),
            make_tile(lengths_ref, rows, met, ((1, me - 2),)),
        ]

    def last():
        return odd(((2, me + 1),))

    return even, odd, last


def by_place(third, me, plan_of, run):
    odd = lax.rem(me, 2) == 1
    even_plan, odd_plan, last_plan = plan_of
    pl.when(lax.rem(me, 2) == 0)(lambda: run("even", even_plan()))
    if third is None:
        pl.when(odd)(lambda: run("odd", odd_plan()))
    else:
        pl.when(odd & (me != third))(lambda: run("odd", odd_plan()))
        pl.when(me == third)(lambda: run("third", last_plan()))


def at_start(step, refs):
    @pl.when(step == 0)
    def _():
        for ref in refs:
            ref[...] = jnp.zeros_like(ref)


def lane_cut(value, number, rows):
    return value[:, number * rows : (number + 1) * rows]


def row_of(group, kinds, kind, head):
    return pl.ds((group * kinds + kind) * GROUP + head, 1)


def per_query(slots, kinds, kind, head, ref):
    return stack([ref[row_of(slot, kinds, kind, head), :] for slot in slots], 1)


def stats_kernel(third, heads, power, place_ref, lengths_ref, *refs):
    count = 2 if third is None else 3
    query_refs, (k_own, k_back, o_own, v_own) = refs[:count], refs[count : count + 4]
    o_copy, v_copy, out_ref = refs[-3:]
    rows, me, step = k_own.shape[1], place_ref[0], pl.program_id(0)
    at_start(step, [out_ref])
    o_copy[...], v_copy[...] = o_own[...], v_own[...]
    queries, keys = [(ref,) for ref in query_refs], ((k_own,), (k_back,))

    def run(_, plan):
        for head, (tiles, _) in tiles_ahead(heads, plan, queries, keys, 1):
            parts = {}
            for (query_slots, _, mask), (_, _, (raw,)) in zip(plan, tiles):
                raw = jnp.where(mask, raw, FLOOR)
                for number, slot in enumerate(query_slots):
                    parts.setdefault(slot, []).append(lane_cut(raw, number, rows))
            for slot, pieces in parts.items():
                top = functools.reduce(
                    jnp.maximum, [jnp.max(p, axis=0, keepdims=True) for p in pieces]
                )
                sums = sum(
                    jnp.sum(jnp.exp2((p - top) * power), axis=0, keepdims=True) for p in pieces
                )
                out_ref[row_of(slot, 2, 0, step * heads + head), :] = top
                out_ref[row_of(slot, 2, 1, step * heads + head), :] = sums

    by_place(third, me, plans(third, lengths_ref, rows, me), run)


def group_parts(third, place, kinds, mine, messages):
    size = kinds * GROUP

    def group(ref, number):
        return ref[number * size : (number + 1) * size, :]

    own = [group(mine, 0), group(messages[0], 1)]
    mate = [group(mine, 1), group(messages[0], 0)]
    if third is None:
        return [own, mate]
    _, near, far = messages
    if place == "even":
        return [own + [group(near, 2)], mate]
    if place == "odd":
        return [own, mate + [group(far, 2)]]
    return [own, mate, [group(mine, 2), group(near, 0), group(far, 1)]]


def merge_stats(scaling, parts):
    split = [(jnp.where(p[GROUP:] > 0, p[:GROUP], FLOOR), p[GROUP:]) for p in parts]
    top = functools.reduce(jnp.maximum, [s[0] for s in split])
    total = sum(jnp.exp((s[0] - top) * scaling) * s[1] for s in split)
    return top + jnp.log(jnp.where(total > 0, total, 1.0)) / scaling


class Emitter:
    def __init__(self, outs):
        self.outs, self.carry = outs, {}

    def emit(self, head, name, value):
        ref = self.outs[name]
        low, high = head_span(head)
        first, last = head * HEAD % LANES == 0, (head + 1) * HEAD % LANES == 0
        start, stop = low, high
        if not first:
            shared = value[:, :LANES] + self.carry.pop(name)
            ref[0, :, low : low + LANES] = shared.astype(jnp.bfloat16)
            start = low + LANES
        if not last:
            self.carry[name] = value[:, high - LANES - low :]
            stop = high - LANES
        if stop > start:
            ref[0, :, start:stop] = value[:, start - low : stop - low].astype(jnp.bfloat16)


def add_rows(sums, kind, slots, value, rows):
    for number, slot in enumerate(slots):
        piece = value[number * rows : (number + 1) * rows]
        name = (kind, slot)
        sums[name] = sums[name] + piece if name in sums else piece


def add_lanes(sums, slots, value, rows):
    for number, slot in enumerate(slots):
        piece = lane_cut(value, number, rows)
        sums[slot] = sums[slot] + piece if slot in sums else piece


def split_refs(third, refs):
    count = 2 if third is None else 3
    queries = [(refs[2 * n], refs[2 * n + 1]) for n in range(count)]
    keys = [(refs[2 * n], refs[2 * n + 1]) for n in range(count, count + 2)]
    return queries, keys, refs[2 * count + 4 :]


def values_kernel(third, heads, scaling, power, place_ref, lengths_ref, *refs):
    count, messages = (2, 1) if third is None else (3, 3)
    queries = [(refs[2 * n], refs[2 * n + 1]) for n in range(count)]
    refs = refs[2 * count :]
    keys, mine, others = [(refs[0],), (refs[1],)], refs[2], refs[3 : 3 + messages]
    value_own, value_back, shift_ref = refs[3 + messages :]
    rows, me, step = keys[0][0].shape[1], place_ref[0], pl.program_id(0)

    def run(place, plan):
        groups = group_parts(third, place, 2, mine, others)
        for number, parts in enumerate(groups):
            shift_ref[number * GROUP : (number + 1) * GROUP, :] = merge_stats(scaling, parts)
        out = Emitter({("v", 0): value_own, ("v", 1): value_back})
        for head, (tiles, keep) in tiles_ahead(heads, plan, queries, keys, 1):
            low, high = head_span(head)
            sums = {}
            for (query_slots, key_slots, mask), (_, _, (raw,)) in zip(plan, tiles):
                shift = per_query(query_slots, 1, 0, step * heads + head, shift_ref)
                weight = jnp.where(mask, jnp.exp2((raw - shift) * power), 0.0).astype(jnp.bfloat16)
                o = stack([queries[slot][1][0, :, low:high] for slot in query_slots], 0) * keep
                add_rows(sums, "v", key_slots, matmul(weight, o, NN), rows)
            for name, value in sums.items():
                out.emit(head, name, value)

    by_place(third, me, plans(third, lengths_ref, rows, me), run)


def dots_kernel(third, heads, power, place_ref, lengths_ref, *refs):
    queries, keys, (shift_ref, dots_ref) = split_refs(third, refs)
    rows, me, step = keys[0][0].shape[1], place_ref[0], pl.program_id(0)
    at_start(step, [dots_ref])

    def run(_, plan):
        for head, (tiles, _) in tiles_ahead(heads, plan, queries, keys, 2):
            at = step * heads + head
            dots = {}
            for (query_slots, _, mask), (_, _, (raw, grads)) in zip(plan, tiles):
                shift = per_query(query_slots, 1, 0, at, shift_ref)
                weight = jnp.where(mask, jnp.exp2((raw - shift) * power), 0.0)
                add_lanes(dots, query_slots, jnp.sum(weight * grads, axis=0, keepdims=True), rows)
            for slot, value in dots.items():
                dots_ref[row_of(slot, 1, 0, at), :] = value

    by_place(third, me, plans(third, lengths_ref, rows, me), run)


def keys_kernel(third, heads, scaling, power, place_ref, lengths_ref, *refs):
    queries, keys, refs = split_refs(third, refs)
    messages = 1 if third is None else 3
    shift_ref, mine, others = refs[0], refs[1], refs[2 : 2 + messages]
    key_own, key_back, *query_refs, total_ref = refs[2 + messages :]
    rows, me, step = keys[0][0].shape[1], place_ref[0], pl.program_id(0)

    def run(place, plan):
        for number, parts in enumerate(group_parts(third, place, 1, mine, others)):
            total_ref[number * GROUP : (number + 1) * GROUP, :] = sum(parts)
        outs = {("k", 0): key_own, ("k", 1): key_back}
        outs.update({("q", slot): ref for slot, ref in enumerate(query_refs)})
        out = Emitter(outs)
        for head, (tiles, keep) in tiles_ahead(heads, plan, queries, keys, 2):
            at = step * heads + head
            sums = {}
            for (query_slots, key_slots, mask), ((q, _), (k, _), (raw, grads)) in zip(plan, tiles):
                shift = per_query(query_slots, 1, 0, at, shift_ref)
                dots = per_query(query_slots, 1, 0, at, total_ref)
                weight = jnp.where(mask, jnp.exp2((raw - shift) * power), 0.0)
                slope = (weight * (grads - dots) * scaling).astype(jnp.bfloat16)
                add_rows(sums, "k", key_slots, matmul(slope, q * keep, NN), rows)
                add_rows(sums, "q", query_slots, matmul(slope, k, TN), rows)
            for name, value in sums.items():
                out.emit(head, name, value)

    by_place(third, me, plans(third, lengths_ref, rows, me), run)


def halo_program(third, queries, key_vectors, value_vectors, out_grad, doc_lengths):
    _, rows, width = queries.shape
    seq_size = lax.axis_size("seq")
    me = lax.axis_index("seq").astype(jnp.int32)
    scaling = HEAD ** (-0.5)
    power = scaling * math.log2(math.e)
    steps = width // HEAD // 4
    part = width // steps
    heads = part // HEAD
    count = 2 if third is None else 3
    devices = range(seq_size)
    mates = [(s, s ^ 1) for s in devices]
    ring = third is None
    ahead = [(s, (s + 2) % seq_size) for s in devices if ring or s + 2 < seq_size]
    behind = [(s, (s - 2) % seq_size) for s in devices if ring or s >= 2]
    if not ring:
        relay, to_even = [(third + 2, third)], [(third, third + 1)]
        near, far = (to_even + [(third + 1, third)], relay + [(third, third + 2)])

    def send(value, pairs):
        return lax.ppermute(value, "seq", pairs)

    def exchange(value):
        return [send(value, pairs) for pairs in ([mates] if ring else [mates, near, far])]

    smem = pl.BlockSpec(memory_space=pltpu.SMEM)
    wide = pl.BlockSpec((1, rows, part), lambda step: (0, 0, step))
    wide_shape = jax.ShapeDtypeStruct((1, rows, width), jnp.bfloat16)

    def slim(kinds):
        return pl.BlockSpec((count * kinds * GROUP, rows), lambda step: (0, 0))

    def slim_shape(kinds):
        return jax.ShapeDtypeStruct((count * kinds * GROUP, rows), jnp.float32)

    def call(kernel, products, wides, slims, outs, slim_outs, scratch=(), after=()):
        flops = 2 * products * 4 * rows * rows * width * 3 // 2
        return pl.pallas_call(
            kernel,
            grid=(steps,),
            in_specs=[smem, smem]
            + [wide] * len(wides)
            + [slim(kinds) for kinds, _ in slims]
            + [pl.BlockSpec(memory_space=pl.ANY)] * len(after),
            out_specs=[wide] * outs + [slim(kinds) for kinds in slim_outs],
            out_shape=[wide_shape] * outs + [slim_shape(kinds) for kinds in slim_outs],
            scratch_shapes=scratch,
            compiler_params=pltpu.CompilerParams(vmem_limit_bytes=20 * 1024 * 1024),
            cost_estimate=pl.CostEstimate(
                flops=flops, bytes_accessed=20 * rows * width, transcendentals=0
            ),
        )(me[None], doc_lengths, *wides, *[value for _, value in slims], *after)

    query_mate = send(queries, mates)
    key_back = send(key_vectors, ahead)
    grad_mate = send(out_grad, mates)
    value_back = send(value_vectors, ahead)
    query_rows = [queries, query_mate] + ([] if ring else [send(query_mate, relay)])
    grad_own, value_own, stats = call(
        functools.partial(stats_kernel, third, heads, power), 1,
        [*query_rows, key_vectors, key_back, out_grad, value_vectors], [], 2, [2],
        after=[] if ring else [value_back],
    )
    grad_rows = [grad_own, grad_mate] + ([] if ring else [send(grad_mate, relay)])
    tensors = [t for two in zip(query_rows, grad_rows) for t in two]
    tensors += [key_vectors, value_own, key_back, value_back]
    value_part, value_sent, shift = call(
        functools.partial(values_kernel, third, heads, scaling, power), 2,
        tensors[: 2 * count] + [key_vectors, key_back],
        [(2, value) for value in [stats] + exchange(stats)], 2, [1],
    )
    (dots,) = call(
        functools.partial(dots_kernel, third, heads, power), 2, tensors, [(1, shift)], 0, [1]
    )
    value_received = send(value_sent, behind)
    key_part, key_sent, query_part, *query_sent = call(
        functools.partial(keys_kernel, third, heads, scaling, power), 4, tensors,
        [(1, value) for value in [shift, dots] + exchange(dots)], 2 + count, [],
        [pltpu.VMEM((count * GROUP, rows), jnp.float32)],
    )
    key_received = send(key_sent, behind)
    query_received = [send(value, pairs) for value, pairs in zip(query_sent, (mates,) if ring else (mates, to_even))]

    def total(*terms):
        return sum(term.astype(jnp.float32) for term in terms).astype(jnp.bfloat16)

    return (
        total(query_part, *query_received),
        total(key_part, key_received),
        total(value_part, value_received),
    )


def program_index(rows, doc_lengths):
    count = doc_lengths.shape[0]
    ends = sum(lax.pad(doc_lengths[: count - n], jnp.int32(0), [(n, 0, 0)]) for n in range(count))
    shift = rows.bit_length() - 1
    first, last = (ends - doc_lengths) >> shift, (ends - 1) >> shift
    spans = (last - first >= 3) & (last & 1 == 0)
    return jnp.sum(jnp.where(spans, (last >> 1) - 1, 0))


def halo_shards(*arguments):
    rows, doc_lengths = arguments[0].shape[1], arguments[-1]
    thirds = range(3, lax.axis_size("seq") - 2, 2)
    programs = [functools.partial(halo_program, third) for third in (None, *thirds)]
    return lax.switch(program_index(rows, doc_lengths), programs, *arguments)


def shards(queries, key_vectors, value_vectors, out_grad, doc_lengths):
    _, rows, width = queries.shape
    seq_size = lax.axis_size("seq")
    longest = rows * seq_size * 3 // 8
    fits = longest <= 3 * rows and seq_size % 2 == 0 and seq_size > 4 and rows == LANES
    heads = width // HEAD
    plan = halo_shards if fits and heads % 4 == 0 and heads <= GROUP else spread_shards
    return plan(queries, key_vectors, value_vectors, out_grad, doc_lengths)


def solution(mesh):
    return jax.shard_map(
        shards,
        mesh=mesh,
        in_specs=(
            P("section", "seq", "dp"),
            P("section", "seq", "dp"),
            P("section", "seq", "dp"),
            P("section", "seq", "dp"),
            P(),
        ),
        out_specs=(P("section", "seq", "dp"), P("section", "seq", "dp"), P("section", "seq", "dp")),
        check_vma=False,
    )
```

profile of v0, /device:TPU:0, one launch (start us, length us, event | category | flops | bytes accessed | tf_op | source)
XLA Modules:
  0.0 54.0 jit_solution(14123485626672014552)
XLA Ops:
  0.6 0.6 %copy-done.6 = s32[8]{0:T(128)S(1)} copy-done((s32[8]{0:T(128)S(1)}, s32[8]{0:T(128)}, u32[]{:S(2)}) %copy-start.6) | copy-done | bytes 56
  1.3 0.7 %fusion = s32[]{:T(128)} fusion(s32[8]{0:T(128)S(1)} %copy-done.6, s32[1]{0:T(128)S(1)} %bitcast.10, s32[2]{0:T(128)S(1)} %bitcast.11, s32[3]{0:T(128)S(1)} %bitcast.12, s32[4]{0:T(128)S(1)} %bitcast.13, s32[5]{0:T(128)S(1)} %bitcast.14, s32[6]{0:T(128)S(1)} %bitcast.15, s32[7]{0:T(128)S(1)} %bitcast.16), kind=kLoop, calls=%fused_computation.10 | loop fusion | flops 159 | bytes 148 | tf_op jit(solution)/shard_map/reduce_sum | solution.py:552
  2.7 51.4 %conditional.4 = (bf16[1,128,1792]{2,1,0:T(8,128)(2,1)}, bf16[1,128,1792]{2,1,0:T(8,128)(2,1)}, bf16[1,128,1792]{2,1,0:T(8,128)(2,1)}) conditional(s32[]{:T(128)} %clamp.3, (bf16[1,128,1792]{2,1,0:T(8,128)(2,1)}, bf16[1,128,1792]{2,1,0:T(8,128)(2,1)}, s32[8]{0:T(128)S(1)}, bf16[1,128,1792]{2,1,0:T(8,128)(2,1)}, ...), branch_computations={%region_1.2_spmd, %region_2.3_spmd, %region_3.4_spmd} | conditional | flops 3174105088 | bytes 45400816
  2.7 3.0 %collective-permute-start = (bf16[1,128,1792]{2,1,0:T(8,128)(2,1)}, bf16[1,128,1792]{2,1,0:T(8,128)(2,1)S(1)}, u32[]{:S(2)}, u32[]{:S(2)}) collective-permute-start(bf16[1,128,1792]{2,1,0:T(8,128)(2,1)} %get-tuple-element.49.refs_0_), channel_id=1, source_target_pairs={{0,4},{4,0},{8,12},{12,8},{16,20},{20,16},{24,28},{28,24},{1,5},{5... | collective-permute-start | bytes 1376264 | tf_op jit(solution)/shard_map/cond/branch_0_fun/ppermute | solution.py:473
  5.7 1.6 %collective-permute-start.1 = (bf16[1,128,1792]{2,1,0:T(8,128)(2,1)}, bf16[1,128,1792]{2,1,0:T(8,128)(2,1)S(1)}, u32[]{:S(2)}, u32[]{:S(2)}) collective-permute-start(bf16[1,128,1792]{2,1,0:T(8,128)(2,1)} %get-tuple-element.50.refs_2_.refs_4_), channel_id=1, source_target_pairs={{0,8},{4,12},{8,16},{12,20},{16,24},{20,28},{24,0},{28,4},{1,9},{5... | collective-permute-start | bytes 1376264 | tf_op jit(solution)/shard_map/cond/branch_0_fun/ppermute | solution.py:473
  7.3 0.5 collective-permute-start.2
  7.8 1.6 %collective-permute-start.3 = (bf16[1,128,1792]{2,1,0:T(8,128)(2,1)}, bf16[1,128,1792]{2,1,0:T(8,128)(2,1)S(1)}, u32[]{:S(2)}, u32[]{:S(2)}) collective-permute-start(bf16[1,128,1792]{2,1,0:T(8,128)(2,1)} %get-tuple-element.52.refs_5_), channel_id=1, source_target_pairs={{0,8},{4,12},{8,16},{12,20},{16,24},{20,28},{24,0},{28,4},{1,9},{5... | collective-permute-start | bytes 1376264 | tf_op jit(solution)/shard_map/cond/branch_0_fun/ppermute | solution.py:473
  9.4 7.9 %collective-permute-done.refs_1_.refs_2_ = bf16[1,128,1792]{2,1,0:T(8,128)(2,1)S(1)} collective-permute-done((bf16[1,128,1792]{2,1,0:T(8,128)(2,1)}, bf16[1,128,1792]{2,1,0:T(8,128)(2,1)S(1)}, u32[]{:S(2)}, u32[]{:S(2)}) %collective-permute-start) | collective-permute-done | bytes 458784 | tf_op jit(solution)/shard_map/cond/branch_0_fun/ppermute | solution.py:473
  17.3 3.9 %collective-permute-done.1.refs_3_.refs_5_.refs_6_ = bf16[1,128,1792]{2,1,0:T(8,128)(2,1)S(1)} collective-permute-done((bf16[1,128,1792]{2,1,0:T(8,128)(2,1)}, bf16[1,128,1792]{2,1,0:T(8,128)(2,1)S(1)}, u32[]{:S(2)}, u32[]{:S(2)}) %collective-permute-start.1) | collective-permute-done | bytes 458784 | tf_op jit(solution)/shard_map/cond/branch_0_fun/ppermute | solution.py:473
  21.2 2.6 %branch_0_fun.4 = (bf16[1,128,1792]{2,1,0:T(8,128)(2,1)S(1)}, bf16[1,128,1792]{2,1,0:T(8,128)(2,1)S(1)}, f32[32,128]{1,0:T(8,128)S(1)}) custom-call(s32[1]{0:T(128)} %bitcast.place_ref, s32[8]{0:T(128)S(1)} %get-tuple-element.48.lengths_ref, bf16[1,128,1792]{2,1,0:T(8,128)(2,1)} %get-tuple-element.49.refs_0_, ...), custom_call_target="tpu_custom_call" | custom-call | flops 352321536 | bytes 4587520 | tf_op jit(solution)/shard_map/cond/branch_0_fun/pallas_call | solution.py:490
  24.2 2.3 %collective-permute-done.2.refs_3_ = bf16[1,128,1792]{2,1,0:T(8,128)(2,1)S(1)} collective-permute-done((bf16[1,128,1792]{2,1,0:T(8,128)(2,1)}, bf16[1,128,1792]{2,1,0:T(8,128)(2,1)S(1)}, u32[]{:S(2)}, u32[]{:S(2)}) %collective-permute-start.2) | collective-permute-done | bytes 458784 | tf_op jit(solution)/shard_map/cond/branch_0_fun/ppermute | solution.py:473
  26.4 1.2 %collective-permute-done.4.refs_7_ = f32[32,128]{1,0:T(8,128)S(1)} collective-permute-done((f32[32,128]{1,0:T(8,128)S(1)}, f32[32,128]{1,0:T(8,128)S(1)}, u32[]{:S(2)}, u32[]{:S(2)}) %collective-permute-start.4) | collective-permute-done | bytes 16416 | tf_op jit(solution)/shard_map/cond/branch_0_fun/ppermute | solution.py:473
  27.6 2.3 %branch_0_fun.5 = (bf16[1,128,1792]{2,1,0:T(8,128)(2,1)S(1)}, bf16[1,128,1792]{2,1,0:T(8,128)(2,1)S(1)}, f32[16,128]{1,0:T(8,128)S(1)}) custom-call(s32[1]{0:T(128)} %bitcast.place_ref, s32[8]{0:T(128)S(1)} %get-tuple-element.48.lengths_ref, bf16[1,128,1792]{2,1,0:T(8,128)(2,1)S(1)} %copy-done, bf16[1,128,1792]{2,1,0:T(8,128)(2,1)S(1)} %get-tuple-element.53.refs_1_, ...), custom_call_target="tpu_custom_call" | custom-call | flops 704643072 | bytes 4587520 | tf_op jit(solution)/shard_map/cond/branch_0_fun/pallas_call | solution.py:490
  29.9 2.9 %collective-permute-start.8 = (bf16[1,128,1792]{2,1,0:T(8,128)(2,1)S(1)}, bf16[1,128,1792]{2,1,0:T(8,128)(2,1)S(1)}, u32[]{:S(2)}, u32[]{:S(2)}) collective-permute-start(bf16[1,128,1792]{2,1,0:T(8,128)(2,1)S(1)} %get-tuple-element.62), channel_id=1, source_target_pairs={{0,24},{4,28},{8,0},{12,4},{16,8},{20,12},{24,16},{28,20},{1,25},{... | collective-permute-start | bytes 1376264 | tf_op jit(solution)/shard_map/cond/branch_0_fun/ppermute | solution.py:473
  32.8 2.1 %branch_0_fun.6.refs_9_ = f32[16,128]{1,0:T(8,128)S(1)} custom-call(s32[1]{0:T(128)} %bitcast.place_ref, s32[8]{0:T(128)S(1)} %get-tuple-element.48.lengths_ref, bf16[1,128,1792]{2,1,0:T(8,128)(2,1)S(1)} %copy-done, bf16[1,128,1792]{2,1,0:T(8,128)(2,1)S(1)} %get-tuple-element.53.refs_1_, bf16[1,128,1792]{2,1,0:T(8,128)(2,1)S(1)} %collective-permute-done.refs_1_.refs_2_, ...), custom_call_target="tpu_custom_call" | custom-call | flops 704643072 | bytes 4587520 | tf_op jit(solution)/shard_map/cond/branch_0_fun/pallas_call | solution.py:490
  34.9 2.0 %collective-permute-start.5 = (f32[16,128]{1,0:T(8,128)S(1)}, f32[16,128]{1,0:T(8,128)S(1)}, u32[]{:S(2)}, u32[]{:S(2)}) collective-permute-start(f32[16,128]{1,0:T(8,128)S(1)} %branch_0_fun.6.refs_9_), channel_id=1, source_target_pairs={{0,4},{4,0},{8,12},{12,8},{16,20},{20,16},{24,28},{28,24},{1,5},{5... | collective-permute-start | bytes 24584 | tf_op jit(solution)/shard_map/cond/branch_0_fun/ppermute | solution.py:473
  36.9 1.7 %collective-permute-done.5.refs_10_ = f32[16,128]{1,0:T(8,128)S(1)} collective-permute-done((f32[16,128]{1,0:T(8,128)S(1)}, f32[16,128]{1,0:T(8,128)S(1)}, u32[]{:S(2)}, u32[]{:S(2)}) %collective-permute-start.5) | collective-permute-done | bytes 8224 | tf_op jit(solution)/shard_map/cond/branch_0_fun/ppermute | solution.py:473
  38.6 3.2 %branch_0_fun.7 = (bf16[1,128,1792]{2,1,0:T(8,128)(2,1)S(1)}, bf16[1,128,1792]{2,1,0:T(8,128)(2,1)S(1)}, bf16[1,128,1792]{2,1,0:T(8,128)(2,1)S(1)}, bf16[1,128,1792]{2,1,0:T(8,128)(2,1)S(1)}) custom-call(s32[1]{0:T(128)} %bitcast.place_ref, s32[8]{0:T(128)S(1)} %get-tuple-element.48.lengths_ref, bf16[1,128,1792]{2,1,0:T(8,128)(2,1)S(1)} %copy-done, ...), custom_call_target="tpu_custom_call" | custom-call | flops 1409286144 | bytes 4587520 | tf_op jit(solution)/shard_map/cond/branch_0_fun/pallas_call | solution.py:490
  41.9 0.5 collective-permute-start.7
  42.3 2.3 %collective-permute-start.6 = (bf16[1,128,1792]{2,1,0:T(8,128)(2,1)S(1)}, bf16[1,128,1792]{2,1,0:T(8,128)(2,1)S(1)}, u32[]{:S(2)}, u32[]{:S(2)}) collective-permute-start(bf16[1,128,1792]{2,1,0:T(8,128)(2,1)S(1)} %get-tuple-element.58), channel_id=1, source_target_pairs={{0,4},{4,0},{8,12},{12,8},{16,20},{20,16},{24,28},{28,24},{1,5},{5... | collective-permute-start | bytes 1376264 | tf_op jit(solution)/shard_map/cond/branch_0_fun/ppermute | solution.py:473
  44.6 0.9 %convert_add_fusion = bf16[1,128,1792]{2,1,0:T(8,128)(2,1)} fusion(bf16[1,128,1792]{2,1,0:T(8,128)(2,1)S(1)} %collective-permute-done.8, bf16[1,128,1792]{2,1,0:T(8,128)(2,1)S(1)} %get-tuple-element.61), kind=kLoop, calls=%fused_computation | loop fusion | flops 917504 | bytes 1376256 | tf_op jit(solution)/shard_map/cond/branch_0_fun/add | solution.py:537
  45.5 6.7 %collective-permute-done.7 = bf16[1,128,1792]{2,1,0:T(8,128)(2,1)S(1)} collective-permute-done((bf16[1,128,1792]{2,1,0:T(8,128)(2,1)S(1)}, bf16[1,128,1792]{2,1,0:T(8,128)(2,1)S(1)}, u32[]{:S(2)}, u32[]{:S(2)}) %collective-permute-start.7) | collective-permute-done | bytes 458784 | tf_op jit(solution)/shard_map/cond/branch_0_fun/ppermute | solution.py:473
  52.3 0.9 %convert_add_fusion.1 = bf16[1,128,1792]{2,1,0:T(8,128)(2,1)} fusion(bf16[1,128,1792]{2,1,0:T(8,128)(2,1)S(1)} %collective-permute-done.7, bf16[1,128,1792]{2,1,0:T(8,128)(2,1)S(1)} %get-tuple-element.59), kind=kLoop, calls=%fused_computation.1 | loop fusion | flops 917504 | bytes 1376256 | tf_op jit(solution)/shard_map/cond/branch_0_fun/add | solution.py:537
  53.2 0.9 %convert_add_fusion.2 = bf16[1,128,1792]{2,1,0:T(8,128)(2,1)} fusion(bf16[1,128,1792]{2,1,0:T(8,128)(2,1)S(1)} %collective-permute-done.6, bf16[1,128,1792]{2,1,0:T(8,128)(2,1)S(1)} %get-tuple-element.57), kind=kLoop, calls=%fused_computation.2 | loop fusion | flops 917504 | bytes 1376256 | tf_op jit(solution)/shard_map/cond/branch_0_fun/add | solution.py:537
  (9 shorter events, 0.4 us)
Async XLA Ops:
  0.6 0.7 %copy-start.6 = (s32[8]{0:T(128)S(1)}, s32[8]{0:T(128)}, u32[]{:S(2)}) copy-start(s32[8]{0:T(128)} %param.12) | copy-start | bytes 100
  2.7 14.6 %collective-permute-start = (bf16[1,128,1792]{2,1,0:T(8,128)(2,1)}, bf16[1,128,1792]{2,1,0:T(8,128)(2,1)S(1)}, u32[]{:S(2)}, u32[]{:S(2)}) collective-permute-start(bf16[1,128,1792]{2,1,0:T(8,128)(2,1)} %get-tuple-element.49.refs_0_), channel_id=1, source_target_pairs={{0,4},{4,0},{8,12},{12,8},{16,20},{20,16},{24,28},{28,24},{1,5},{5... | collective-permute-start | bytes 1376264 | tf_op jit(solution)/shard_map/cond/branch_0_fun/ppermute | solution.py:473
  5.7 15.4 %collective-permute-start.1 = (bf16[1,128,1792]{2,1,0:T(8,128)(2,1)}, bf16[1,128,1792]{2,1,0:T(8,128)(2,1)S(1)}, u32[]{:S(2)}, u32[]{:S(2)}) collective-permute-start(bf16[1,128,1792]{2,1,0:T(8,128)(2,1)} %get-tuple-element.50.refs_2_.refs_4_), channel_id=1, source_target_pairs={{0,8},{4,12},{8,16},{12,20},{16,24},{20,28},{24,0},{28,4},{1,9},{5... | collective-permute-start | bytes 1376264 | tf_op jit(solution)/shard_map/cond/branch_0_fun/ppermute | solution.py:473
  7.3 19.2 %collective-permute-start.2 = (bf16[1,128,1792]{2,1,0:T(8,128)(2,1)}, bf16[1,128,1792]{2,1,0:T(8,128)(2,1)S(1)}, u32[]{:S(2)}, u32[]{:S(2)}) collective-permute-start(bf16[1,128,1792]{2,1,0:T(8,128)(2,1)} %get-tuple-element.51.refs_4_), channel_id=1, source_target_pairs={{0,4},{4,0},{8,12},{12,8},{16,20},{20,16},{24,28},{28,24},{1,5},{5... | collective-permute-start | bytes 1376264 | tf_op jit(solution)/shard_map/cond/branch_0_fun/ppermute | solution.py:473
  7.8 25.0 %collective-permute-start.3 = (bf16[1,128,1792]{2,1,0:T(8,128)(2,1)}, bf16[1,128,1792]{2,1,0:T(8,128)(2,1)S(1)}, u32[]{:S(2)}, u32[]{:S(2)}) collective-permute-start(bf16[1,128,1792]{2,1,0:T(8,128)(2,1)} %get-tuple-element.52.refs_5_), channel_id=1, source_target_pairs={{0,8},{4,12},{8,16},{12,20},{16,24},{20,28},{24,0},{28,4},{1,9},{5... | collective-permute-start | bytes 1376264 | tf_op jit(solution)/shard_map/cond/branch_0_fun/ppermute | solution.py:473
  21.2 6.5 %copy-start = (bf16[1,128,1792]{2,1,0:T(8,128)(2,1)S(1)}, bf16[1,128,1792]{2,1,0:T(8,128)(2,1)}, u32[]{:S(2)}) copy-start(bf16[1,128,1792]{2,1,0:T(8,128)(2,1)} %get-tuple-element.49.refs_0_) | copy-start | bytes 1376260
  21.2 6.5 %copy-start.3 = (bf16[1,128,1792]{2,1,0:T(8,128)(2,1)S(1)}, bf16[1,128,1792]{2,1,0:T(8,128)(2,1)}, u32[]{:S(2)}) copy-start(bf16[1,128,1792]{2,1,0:T(8,128)(2,1)} %get-tuple-element.50.refs_2_.refs_4_) | copy-start | bytes 1376260
  23.8 3.8 %collective-permute-start.4 = (f32[32,128]{1,0:T(8,128)S(1)}, f32[32,128]{1,0:T(8,128)S(1)}, u32[]{:S(2)}, u32[]{:S(2)}) collective-permute-start(f32[32,128]{1,0:T(8,128)S(1)} %get-tuple-element.55.refs_6_), channel_id=1, source_target_pairs={{0,4},{4,0},{8,12},{12,8},{16,20},{20,16},{24,28},{28,24},{1,5},{5... | collective-permute-start | bytes 49160 | tf_op jit(solution)/shard_map/cond/branch_0_fun/ppermute | solution.py:473
  29.9 14.7 %collective-permute-start.8 = (bf16[1,128,1792]{2,1,0:T(8,128)(2,1)S(1)}, bf16[1,128,1792]{2,1,0:T(8,128)(2,1)S(1)}, u32[]{:S(2)}, u32[]{:S(2)}) collective-permute-start(bf16[1,128,1792]{2,1,0:T(8,128)(2,1)S(1)} %get-tuple-element.62), channel_id=1, source_target_pairs={{0,24},{4,28},{8,0},{12,4},{16,8},{20,12},{24,16},{28,20},{1,25},{... | collective-permute-start | bytes 1376264 | tf_op jit(solution)/shard_map/cond/branch_0_fun/ppermute | solution.py:473
  34.9 3.7 %collective-permute-start.5 = (f32[16,128]{1,0:T(8,128)S(1)}, f32[16,128]{1,0:T(8,128)S(1)}, u32[]{:S(2)}, u32[]{:S(2)}) collective-permute-start(f32[16,128]{1,0:T(8,128)S(1)} %branch_0_fun.6.refs_9_), channel_id=1, source_target_pairs={{0,4},{4,0},{8,12},{12,8},{16,20},{20,16},{24,28},{28,24},{1,5},{5... | collective-permute-start | bytes 24584 | tf_op jit(solution)/shard_map/cond/branch_0_fun/ppermute | solution.py:473
  41.9 10.4 %collective-permute-start.7 = (bf16[1,128,1792]{2,1,0:T(8,128)(2,1)S(1)}, bf16[1,128,1792]{2,1,0:T(8,128)(2,1)S(1)}, u32[]{:S(2)}, u32[]{:S(2)}) collective-permute-start(bf16[1,128,1792]{2,1,0:T(8,128)(2,1)S(1)} %get-tuple-element.60), channel_id=1, source_target_pairs={{0,24},{4,28},{8,0},{12,4},{16,8},{20,12},{24,16},{28,20},{1,25},{... | collective-permute-start | bytes 1376264 | tf_op jit(solution)/shard_map/cond/branch_0_fun/ppermute | solution.py:473
  42.3 10.8 %collective-permute-start.6 = (bf16[1,128,1792]{2,1,0:T(8,128)(2,1)S(1)}, bf16[1,128,1792]{2,1,0:T(8,128)(2,1)S(1)}, u32[]{:S(2)}, u32[]{:S(2)}) collective-permute-start(bf16[1,128,1792]{2,1,0:T(8,128)(2,1)S(1)} %get-tuple-element.58), channel_id=1, source_target_pairs={{0,4},{4,0},{8,12},{12,8},{16,20},{20,16},{24,28},{28,24},{1,5},{5... | collective-permute-start | bytes 1376264 | tf_op jit(solution)/shard_map/cond/branch_0_fun/ppermute | solution.py:473
where the time goes:
time: 54.2 us; the launch traced here: 54 us
  waiting for transfers between devices  23.7 us (44%)
  starting transfers between devices  14.7 us (27%)
  Pallas kernels  10.2 us (19%)
  other arithmetic  3.4 us (6%)
  between operations  1.29 us (2%)
  local copies, waits for them, and re-layouts  0.66 us (1%)
    ppermute x9, waiting for transfers between devices, send(): return lax.ppermute(value, 'seq', pairs)  23.7 us
    ppermute x9, starting transfers between devices, send(): return lax.ppermute(value, 'seq', pairs)  14.7 us
    pallas_call x4, Pallas kernels, call(): pl.pallas_call(kernel, grid=(steps,), in_specs=[smem, smem] + [wide] * le...  10.2 us
    add x3, other arithmetic, total(): sum((term.astype(jnp.float32) for term in terms)).astype(jnp.bfloat16)  2.65 us
  transfers between devices with their start and end apart: 9, of which 6 were waited for; matrix products, arithmetic and copies ran while one was open for 3% of the time, Pallas kernels for 19%

commit v1 on v0

--- a/solution.py
+++ b/solution.py
@@ -450,6 +450,13 @@
     by_place(third, me, plans(third, lengths_ref, rows, me), run)
 
 
+def sums_kernel(counts, *refs):
+    outs = refs[sum(counts) :]
+    for count, out in zip(counts, outs):
+        terms, refs = refs[:count], refs[count:]
+        out[...] = sum(ref[...].astype(jnp.float32) for ref in terms).astype(jnp.bfloat16)
+
+
 def halo_program(third, queries, key_vectors, value_vectors, out_grad, doc_lengths):
     _, rows, width = queries.shape
     seq_size = lax.axis_size("seq")
@@ -463,7 +470,8 @@
     devices = range(seq_size)
     mates = [(s, s ^ 1) for s in devices]
     ring = third is None
-    ahead = [(s, (s + 2) % seq_size) for s in devices if ring or s + 2 < seq_size]
+    chain = [(s, s + 2) for s in devices if s + 2 < seq_size]
+    ahead = [(s, (s + 2) % seq_size) for s in devices] if ring else chain
     behind = [(s, (s - 2) % seq_size) for s in devices if ring or s >= 2]
     if not ring:
         relay, to_even = [(third + 2, third)], [(third, third + 1)]
@@ -504,7 +512,7 @@
         )(me[None], doc_lengths, *wides, *[value for _, value in slims], *after)
 
     query_mate = send(queries, mates)
-    key_back = send(key_vectors, ahead)
+    key_back = send(key_vectors, chain)
     grad_mate = send(out_grad, mates)
     value_back = send(value_vectors, ahead)
     query_rows = [queries, query_mate] + ([] if ring else [send(query_mate, relay)])
@@ -533,14 +541,23 @@
     key_received = send(key_sent, behind)
     query_received = [send(value, pairs) for value, pairs in zip(query_sent, (mates,) if ring else (mates, to_even))]
 
-    def total(*terms):
-        return sum(term.astype(jnp.float32) for term in terms).astype(jnp.bfloat16)
-
-    return (
-        total(query_part, *query_received),
-        total(key_part, key_received),
-        total(value_part, value_received),
-    )
+    def total(groups):
+        flat = [term for terms in groups for term in terms]
+        return pl.pallas_call(
+            functools.partial(sums_kernel, [len(terms) for terms in groups]),
+            grid=(steps,),
+            in_specs=[wide] * len(flat),
+            out_specs=[wide] * len(groups),
+            out_shape=[wide_shape] * len(groups),
+            compiler_params=pltpu.CompilerParams(vmem_limit_bytes=20 * 1024 * 1024),
+            cost_estimate=pl.CostEstimate(
+                flops=rows * width, bytes_accessed=8 * rows * width, transcendentals=0
+            ),
+        )(*flat)
+
+    (value_ready,) = total([[value_part, value_received]])
+    key_ready, query_ready = total([[key_part, key_received], [query_part, *query_received]])
+    return query_ready, key_ready, value_ready
 
 
 def program_index(rows, doc_lengths):

time: 54.2 us -> 56.7 us (1.046)
  starting transfers between devices: 14.7 us -> 18.9 us
  other arithmetic: 3.4 us -> 0.75 us
  Pallas kernels: 10.2 us -> 12.3 us
  waiting for transfers between devices: 23.7 us -> 22.5 us
    ppermute x9, starting transfers between devices: 14.7 us -> 18.9 us  [send(): return lax.ppermute(value, 'seq', pairs)]
    add x3 -> x0, other arithmetic: 2.65 us -> none  [total(): sum((term.astype(jnp.float32) for term in terms)).astype(jnp.bfloat16)]
    pallas_call x0 -> x2, Pallas kernels: none -> 2.07 us  [total(): pl.pallas_call(functools.partial(sums_kernel, [len(terms) for terms in gr...]
    ppermute x9, waiting for transfers between devices: 23.7 us -> 22.5 us  [send(): return lax.ppermute(value, 'seq', pairs)]
  transfers between devices with their start and end apart: 9 -> 9, of which waited for: 6 -> 6; matrix products, arithmetic and copies ran while one was open for 3% -> 0% of each run, Pallas kernels for 19% -> 16%
where the time goes in v1:
time: 56.7 us; the launch traced here: 56.5 us
  waiting for transfers between devices  22.5 us (40%)
  starting transfers between devices  18.9 us (33%)
  Pallas kernels  12.3 us (22%)
  between operations  1.29 us (2%)
  other arithmetic  0.75 us (1%)
  local copies, waits for them, and re-layouts  0.66 us (1%)
    ppermute x9, waiting for transfers between devices, send(): return lax.ppermute(value, 'seq', pairs)  22.5 us
    ppermute x9, starting transfers between devices, send(): return lax.ppermute(value, 'seq', pairs)  18.9 us
    pallas_call x4, Pallas kernels, call(): pl.pallas_call(kernel, grid=(steps,), in_specs=[smem, smem] + [wide] * le...  10.2 us
    pallas_call x2, Pallas kernels, total(): pl.pallas_call(functools.partial(sums_kernel, [len(terms) for terms in gr...  2.07 us
  transfers between devices with their start and end apart: 9, of which 6 were waited for; matrix products, arithmetic and copies ran while one was open for 0% of the time, Pallas kernels for 16%

profile of v1, /device:TPU:0, one launch (start us, length us, event | category | flops | bytes accessed | tf_op | source)
XLA Modules:
  0.0 56.5 jit_solution(4288813900375743718)
XLA Ops:
  0.6 0.6 %copy-done.6 = s32[8]{0:T(128)S(1)} copy-done((s32[8]{0:T(128)S(1)}, s32[8]{0:T(128)}, u32[]{:S(2)}) %copy-start.6) | copy-done | bytes 56
  1.3 0.7 %fusion = s32[]{:T(128)} fusion(s32[8]{0:T(128)S(1)} %copy-done.6, s32[1]{0:T(128)S(1)} %bitcast.10, s32[2]{0:T(128)S(1)} %bitcast.11, s32[3]{0:T(128)S(1)} %bitcast.12, s32[4]{0:T(128)S(1)} %bitcast.13, s32[5]{0:T(128)S(1)} %bitcast.14, s32[6]{0:T(128)S(1)} %bitcast.15, s32[7]{0:T(128)S(1)} %bitcast.16), kind=kLoop, calls=%fused_computation.1 | loop fusion | flops 159 | bytes 148 | tf_op jit(solution)/shard_map/reduce_sum | solution.py:569
  2.7 53.8 %conditional.1 = (bf16[1,128,1792]{2,1,0:T(8,128)(2,1)}, bf16[1,128,1792]{2,1,0:T(8,128)(2,1)}, bf16[1,128,1792]{2,1,0:T(8,128)(2,1)}) conditional(s32[]{:T(128)} %clamp.3, (bf16[1,128,1792]{2,1,0:T(8,128)(2,1)}, bf16[1,128,1792]{2,1,0:T(8,128)(2,1)}, s32[8]{0:T(128)S(1)}, bf16[1,128,1792]{2,1,0:T(8,128)(2,1)}, ...), branch_computations={%region_1.2_spmd, %region_2.3_spmd, %region_3.4_spmd} | conditional | flops 3171352576 | bytes 44483312 | solution.py:576
  2.7 3.0 %collective-permute-start = (bf16[1,128,1792]{2,1,0:T(8,128)(2,1)}, bf16[1,128,1792]{2,1,0:T(8,128)(2,1)S(1)}, u32[]{:S(2)}, u32[]{:S(2)}) collective-permute-start(bf16[1,128,1792]{2,1,0:T(8,128)(2,1)} %get-tuple-element.31.refs_0_), channel_id=1, source_target_pairs={{0,4},{4,0},{8,12},{12,8},{16,20},{20,16},{24,28},{28,24},{1,5},{5... | collective-permute-start | bytes 1376264 | tf_op jit(solution)/shard_map/cond/branch_0_fun/ppermute | solution.py:481
  5.7 3.5 %collective-permute-start.1 = (bf16[1,128,1792]{2,1,0:T(8,128)(2,1)}, bf16[1,128,1792]{2,1,0:T(8,128)(2,1)S(1)}, u32[]{:S(2)}, u32[]{:S(2)}) collective-permute-start(bf16[1,128,1792]{2,1,0:T(8,128)(2,1)} %get-tuple-element.32.refs_2_.refs_4_), channel_id=1, source_target_pairs={{0,8},{4,12},{8,16},{12,20},{16,24},{20,28},{1,9},{5,13},{9,17},{1... | collective-permute-start | bytes 1376264 | tf_op jit(solution)/shard_map/cond/branch_0_fun/ppermute | solution.py:481
  9.2 0.6 %collective-permute-start.2 = (bf16[1,128,1792]{2,1,0:T(8,128)(2,1)}, bf16[1,128,1792]{2,1,0:T(8,128)(2,1)S(1)}, u32[]{:S(2)}, u32[]{:S(2)}) collective-permute-start(bf16[1,128,1792]{2,1,0:T(8,128)(2,1)} %get-tuple-element.33.refs_4_), channel_id=1, source_target_pairs={{0,4},{4,0},{8,12},{12,8},{16,20},{20,16},{24,28},{28,24},{1,5},{5... | collective-permute-start | bytes 1376264 | tf_op jit(solution)/shard_map/cond/branch_0_fun/ppermute | solution.py:481
  9.8 1.6 %collective-permute-start.3 = (bf16[1,128,1792]{2,1,0:T(8,128)(2,1)}, bf16[1,128,1792]{2,1,0:T(8,128)(2,1)S(1)}, u32[]{:S(2)}, u32[]{:S(2)}) collective-permute-start(bf16[1,128,1792]{2,1,0:T(8,128)(2,1)} %get-tuple-element.34.refs_5_), channel_id=1, source_target_pairs={{0,8},{4,12},{8,16},{12,20},{16,24},{20,28},{24,0},{28,4},{1,9},{5... | collective-permute-start | bytes 1376264 | tf_op jit(solution)/shard_map/cond/branch_0_fun/ppermute | solution.py:481
  11.4 5.9 %collective-permute-done.refs_1_.refs_2_ = bf16[1,128,1792]{2,1,0:T(8,128)(2,1)S(1)} collective-permute-done((bf16[1,128,1792]{2,1,0:T(8,128)(2,1)}, bf16[1,128,1792]{2,1,0:T(8,128)(2,1)S(1)}, u32[]{:S(2)}, u32[]{:S(2)}) %collective-permute-start) | collective-permute-done | bytes 458784 | tf_op jit(solution)/shard_map/cond/branch_0_fun/ppermute | solution.py:481
  17.3 3.2 %collective-permute-done.1.refs_3_.refs_5_.refs_6_ = bf16[1,128,1792]{2,1,0:T(8,128)(2,1)S(1)} collective-permute-done((bf16[1,128,1792]{2,1,0:T(8,128)(2,1)}, bf16[1,128,1792]{2,1,0:T(8,128)(2,1)S(1)}, u32[]{:S(2)}, u32[]{:S(2)}) %collective-permute-start.1) | collective-permute-done | bytes 458784 | tf_op jit(solution)/shard_map/cond/branch_0_fun/ppermute | solution.py:481
  20.4 2.6 %branch_0_fun.6 = (bf16[1,128,1792]{2,1,0:T(8,128)(2,1)S(1)}, bf16[1,128,1792]{2,1,0:T(8,128)(2,1)S(1)}, f32[32,128]{1,0:T(8,128)S(1)}) custom-call(s32[1]{0:T(128)} %bitcast.place_ref, s32[8]{0:T(128)S(1)} %get-tuple-element.30.lengths_ref, bf16[1,128,1792]{2,1,0:T(8,128)(2,1)} %get-tuple-element.31.refs_0_, ...), custom_call_target="tpu_custom_call" | custom-call | flops 352321536 | bytes 4587520 | tf_op jit(solution)/shard_map/cond/branch_0_fun/pallas_call | solution.py:498
  23.1 0.6 %collective-permute-start.4 = (f32[32,128]{1,0:T(8,128)S(1)}, f32[32,128]{1,0:T(8,128)S(1)}, u32[]{:S(2)}, u32[]{:S(2)}) collective-permute-start(f32[32,128]{1,0:T(8,128)S(1)} %get-tuple-element.37.refs_6_), channel_id=1, source_target_pairs={{0,4},{4,0},{8,12},{12,8},{16,20},{20,16},{24,28},{28,24},{1,5},{5... | collective-permute-start | bytes 49160 | tf_op jit(solution)/shard_map/cond/branch_0_fun/ppermute | solution.py:481
  23.7 2.8 %collective-permute-done.2.refs_3_ = bf16[1,128,1792]{2,1,0:T(8,128)(2,1)S(1)} collective-permute-done((bf16[1,128,1792]{2,1,0:T(8,128)(2,1)}, bf16[1,128,1792]{2,1,0:T(8,128)(2,1)S(1)}, u32[]{:S(2)}, u32[]{:S(2)}) %collective-permute-start.2) | collective-permute-done | bytes 458784 | tf_op jit(solution)/shard_map/cond/branch_0_fun/ppermute | solution.py:481
  26.4 0.4 collective-permute-done.4.refs_7_
  26.9 2.3 %branch_0_fun.7 = (bf16[1,128,1792]{2,1,0:T(8,128)(2,1)S(1)}, bf16[1,128,1792]{2,1,0:T(8,128)(2,1)S(1)}, f32[16,128]{1,0:T(8,128)S(1)}) custom-call(s32[1]{0:T(128)} %bitcast.place_ref, s32[8]{0:T(128)S(1)} %get-tuple-element.30.lengths_ref, bf16[1,128,1792]{2,1,0:T(8,128)(2,1)S(1)} %copy-done, bf16[1,128,1792]{2,1,0:T(8,128)(2,1)S(1)} %get-tuple-element.35.refs_1_, ...), custom_call_target="tpu_custom_call" | custom-call | flops 704643072 | bytes 4587520 | tf_op jit(solution)/shard_map/cond/branch_0_fun/pallas_call | solution.py:498
  29.2 2.1 %branch_0_fun.8.refs_9_ = f32[16,128]{1,0:T(8,128)S(1)} custom-call(s32[1]{0:T(128)} %bitcast.place_ref, s32[8]{0:T(128)S(1)} %get-tuple-element.30.lengths_ref, bf16[1,128,1792]{2,1,0:T(8,128)(2,1)S(1)} %copy-done, bf16[1,128,1792]{2,1,0:T(8,128)(2,1)S(1)} %get-tuple-element.35.refs_1_, bf16[1,128,1792]{2,1,0:T(8,128)(2,1)S(1)} %collective-permute-done.refs_1_.refs_2_, ...), custom_call_target="tpu_custom_call" | custom-call | flops 704643072 | bytes 4587520 | tf_op jit(solution)/shard_map/cond/branch_0_fun/pallas_call | solution.py:498
  31.3 1.9 %collective-permute-start.5 = (f32[16,128]{1,0:T(8,128)S(1)}, f32[16,128]{1,0:T(8,128)S(1)}, u32[]{:S(2)}, u32[]{:S(2)}) collective-permute-start(f32[16,128]{1,0:T(8,128)S(1)} %branch_0_fun.8.refs_9_), channel_id=1, source_target_pairs={{0,4},{4,0},{8,12},{12,8},{16,20},{20,16},{24,28},{28,24},{1,5},{5... | collective-permute-start | bytes 24584 | tf_op jit(solution)/shard_map/cond/branch_0_fun/ppermute | solution.py:481
  33.2 3.6 %collective-permute-start.8 = (bf16[1,128,1792]{2,1,0:T(8,128)(2,1)S(1)}, bf16[1,128,1792]{2,1,0:T(8,128)(2,1)S(1)}, u32[]{:S(2)}, u32[]{:S(2)}) collective-permute-start(bf16[1,128,1792]{2,1,0:T(8,128)(2,1)S(1)} %get-tuple-element.46), channel_id=1, source_target_pairs={{0,24},{4,28},{8,0},{12,4},{16,8},{20,12},{24,16},{28,20},{1,25},{... | collective-permute-start | bytes 1376264 | tf_op jit(solution)/shard_map/cond/branch_0_fun/ppermute | solution.py:481
  36.9 3.2 %branch_0_fun.9 = (bf16[1,128,1792]{2,1,0:T(8,128)(2,1)S(1)}, bf16[1,128,1792]{2,1,0:T(8,128)(2,1)S(1)}, bf16[1,128,1792]{2,1,0:T(8,128)(2,1)S(1)}, bf16[1,128,1792]{2,1,0:T(8,128)(2,1)S(1)}) custom-call(s32[1]{0:T(128)} %bitcast.place_ref, s32[8]{0:T(128)S(1)} %get-tuple-element.30.lengths_ref, bf16[1,128,1792]{2,1,0:T(8,128)(2,1)S(1)} %copy-done, ...), custom_call_target="tpu_custom_call" | custom-call | flops 1409286144 | bytes 4587520 | tf_op jit(solution)/shard_map/cond/branch_0_fun/pallas_call | solution.py:498
  40.1 2.6 %collective-permute-start.6 = (bf16[1,128,1792]{2,1,0:T(8,128)(2,1)S(1)}, bf16[1,128,1792]{2,1,0:T(8,128)(2,1)S(1)}, u32[]{:S(2)}, u32[]{:S(2)}) collective-permute-start(bf16[1,128,1792]{2,1,0:T(8,128)(2,1)S(1)} %get-tuple-element.40), channel_id=1, source_target_pairs={{0,24},{4,28},{8,0},{12,4},{16,8},{20,12},{24,16},{28,20},{1,25},{... | collective-permute-start | bytes 1376264 | tf_op jit(solution)/shard_map/cond/branch_0_fun/ppermute | solution.py:481
  42.7 1.5 %collective-permute-start.7 = (bf16[1,128,1792]{2,1,0:T(8,128)(2,1)S(1)}, bf16[1,128,1792]{2,1,0:T(8,128)(2,1)S(1)}, u32[]{:S(2)}, u32[]{:S(2)}) collective-permute-start(bf16[1,128,1792]{2,1,0:T(8,128)(2,1)S(1)} %get-tuple-element.42), channel_id=1, source_target_pairs={{0,4},{4,0},{8,12},{12,8},{16,20},{20,16},{24,28},{28,24},{1,5},{5... | collective-permute-start | bytes 1376264 | tf_op jit(solution)/shard_map/cond/branch_0_fun/ppermute | solution.py:481
  44.2 3.7 %collective-permute-done.8.refs_1_ = bf16[1,128,1792]{2,1,0:T(8,128)(2,1)S(1)} collective-permute-done((bf16[1,128,1792]{2,1,0:T(8,128)(2,1)S(1)}, bf16[1,128,1792]{2,1,0:T(8,128)(2,1)S(1)}, u32[]{:S(2)}, u32[]{:S(2)}) %collective-permute-start.8) | collective-permute-done | bytes 458784 | tf_op jit(solution)/shard_map/cond/branch_0_fun/ppermute | solution.py:481
  47.8 0.9 %branch_0_fun.11 = bf16[1,128,1792]{2,1,0:T(8,128)(2,1)} custom-call(bf16[1,128,1792]{2,1,0:T(8,128)(2,1)S(1)} %get-tuple-element.45.refs_0_, bf16[1,128,1792]{2,1,0:T(8,128)(2,1)S(1)} %collective-permute-done.8.refs_1_), custom_call_target="tpu_custom_call" | custom-call | flops 229376 | bytes 1835008 | tf_op jit(solution)/shard_map/cond/branch_0_fun/pallas_call | solution.py:546
  48.7 6.6 %collective-permute-done.6.refs_1_ = bf16[1,128,1792]{2,1,0:T(8,128)(2,1)S(1)} collective-permute-done((bf16[1,128,1792]{2,1,0:T(8,128)(2,1)S(1)}, bf16[1,128,1792]{2,1,0:T(8,128)(2,1)S(1)}, u32[]{:S(2)}, u32[]{:S(2)}) %collective-permute-start.6) | collective-permute-done | bytes 458784 | tf_op jit(solution)/shard_map/cond/branch_0_fun/ppermute | solution.py:481
  55.3 1.2 %branch_0_fun.10 = (bf16[1,128,1792]{2,1,0:T(8,128)(2,1)}, bf16[1,128,1792]{2,1,0:T(8,128)(2,1)}) custom-call(bf16[1,128,1792]{2,1,0:T(8,128)(2,1)S(1)} %get-tuple-element.39.refs_0_, bf16[1,128,1792]{2,1,0:T(8,128)(2,1)S(1)} %collective-permute-done.6.refs_1_, bf16[1,128,1792]{2,1,0:T(8,128)(2,1)S(1)} %get-tuple-element.41.refs_2_, ...), custom_call_target="tpu_custom_call" | custom-call | flops 229376 | bytes 1835008 | tf_op jit(solution)/shard_map/cond/branch_0_fun/pallas_call | solution.py:546
  (8 shorter events, 0.0 us)
Async XLA Ops:
  0.6 0.7 %copy-start.6 = (s32[8]{0:T(128)S(1)}, s32[8]{0:T(128)}, u32[]{:S(2)}) copy-start(s32[8]{0:T(128)} %param.12) | copy-start | bytes 100
  2.7 14.6 %collective-permute-start = (bf16[1,128,1792]{2,1,0:T(8,128)(2,1)}, bf16[1,128,1792]{2,1,0:T(8,128)(2,1)S(1)}, u32[]{:S(2)}, u32[]{:S(2)}) collective-permute-start(bf16[1,128,1792]{2,1,0:T(8,128)(2,1)} %get-tuple-element.31.refs_0_), channel_id=1, source_target_pairs={{0,4},{4,0},{8,12},{12,8},{16,20},{20,16},{24,28},{28,24},{1,5},{5... | collective-permute-start | bytes 1376264 | tf_op jit(solution)/shard_map/cond/branch_0_fun/ppermute | solution.py:481
  5.7 14.7 %collective-permute-start.1 = (bf16[1,128,1792]{2,1,0:T(8,128)(2,1)}, bf16[1,128,1792]{2,1,0:T(8,128)(2,1)S(1)}, u32[]{:S(2)}, u32[]{:S(2)}) collective-permute-start(bf16[1,128,1792]{2,1,0:T(8,128)(2,1)} %get-tuple-element.32.refs_2_.refs_4_), channel_id=1, source_target_pairs={{0,8},{4,12},{8,16},{12,20},{16,24},{20,28},{1,9},{5,13},{9,17},{1... | collective-permute-start | bytes 1376264 | tf_op jit(solution)/shard_map/cond/branch_0_fun/ppermute | solution.py:481
  9.2 17.2 %collective-permute-start.2 = (bf16[1,128,1792]{2,1,0:T(8,128)(2,1)}, bf16[1,128,1792]{2,1,0:T(8,128)(2,1)S(1)}, u32[]{:S(2)}, u32[]{:S(2)}) collective-permute-start(bf16[1,128,1792]{2,1,0:T(8,128)(2,1)} %get-tuple-element.33.refs_4_), channel_id=1, source_target_pairs={{0,4},{4,0},{8,12},{12,8},{16,20},{20,16},{24,28},{28,24},{1,5},{5... | collective-permute-start | bytes 1376264 | tf_op jit(solution)/shard_map/cond/branch_0_fun/ppermute | solution.py:481
  9.8 19.4 %collective-permute-start.3 = (bf16[1,128,1792]{2,1,0:T(8,128)(2,1)}, bf16[1,128,1792]{2,1,0:T(8,128)(2,1)S(1)}, u32[]{:S(2)}, u32[]{:S(2)}) collective-permute-start(bf16[1,128,1792]{2,1,0:T(8,128)(2,1)} %get-tuple-element.34.refs_5_), channel_id=1, source_target_pairs={{0,8},{4,12},{8,16},{12,20},{16,24},{20,28},{24,0},{28,4},{1,9},{5... | collective-permute-start | bytes 1376264 | tf_op jit(solution)/shard_map/cond/branch_0_fun/ppermute | solution.py:481
  20.4 6.5 %copy-start = (bf16[1,128,1792]{2,1,0:T(8,128)(2,1)S(1)}, bf16[1,128,1792]{2,1,0:T(8,128)(2,1)}, u32[]{:S(2)}) copy-start(bf16[1,128,1792]{2,1,0:T(8,128)(2,1)} %get-tuple-element.31.refs_0_) | copy-start | bytes 1376260 | tf_op jit(solution)/shard_map/cond
  20.4 6.5 %copy-start.3 = (bf16[1,128,1792]{2,1,0:T(8,128)(2,1)S(1)}, bf16[1,128,1792]{2,1,0:T(8,128)(2,1)}, u32[]{:S(2)}) copy-start(bf16[1,128,1792]{2,1,0:T(8,128)(2,1)} %get-tuple-element.32.refs_2_.refs_4_) | copy-start | bytes 1376260 | tf_op jit(solution)/shard_map/cond
  23.1 3.8 %collective-permute-start.4 = (f32[32,128]{1,0:T(8,128)S(1)}, f32[32,128]{1,0:T(8,128)S(1)}, u32[]{:S(2)}, u32[]{:S(2)}) collective-permute-start(f32[32,128]{1,0:T(8,128)S(1)} %get-tuple-element.37.refs_6_), channel_id=1, source_target_pairs={{0,4},{4,0},{8,12},{12,8},{16,20},{20,16},{24,28},{28,24},{1,5},{5... | collective-permute-start | bytes 49160 | tf_op jit(solution)/shard_map/cond/branch_0_fun/ppermute | solution.py:481
  31.3 5.5 %collective-permute-start.5 = (f32[16,128]{1,0:T(8,128)S(1)}, f32[16,128]{1,0:T(8,128)S(1)}, u32[]{:S(2)}, u32[]{:S(2)}) collective-permute-start(f32[16,128]{1,0:T(8,128)S(1)} %branch_0_fun.8.refs_9_), channel_id=1, source_target_pairs={{0,4},{4,0},{8,12},{12,8},{16,20},{20,16},{24,28},{28,24},{1,5},{5... | collective-permute-start | bytes 24584 | tf_op jit(solution)/shard_map/cond/branch_0_fun/ppermute | solution.py:481
  33.2 14.6 %collective-permute-start.8 = (bf16[1,128,1792]{2,1,0:T(8,128)(2,1)S(1)}, bf16[1,128,1792]{2,1,0:T(8,128)(2,1)S(1)}, u32[]{:S(2)}, u32[]{:S(2)}) collective-permute-start(bf16[1,128,1792]{2,1,0:T(8,128)(2,1)S(1)} %get-tuple-element.46), channel_id=1, source_target_pairs={{0,24},{4,28},{8,0},{12,4},{16,8},{20,12},{24,16},{28,20},{1,25},{... | collective-permute-start | bytes 1376264 | tf_op jit(solution)/shard_map/cond/branch_0_fun/ppermute | solution.py:481
  40.1 15.2 %collective-permute-start.6 = (bf16[1,128,1792]{2,1,0:T(8,128)(2,1)S(1)}, bf16[1,128,1792]{2,1,0:T(8,128)(2,1)S(1)}, u32[]{:S(2)}, u32[]{:S(2)}) collective-permute-start(bf16[1,128,1792]{2,1,0:T(8,128)(2,1)S(1)} %get-tuple-element.40), channel_id=1, source_target_pairs={{0,24},{4,28},{8,0},{12,4},{16,8},{20,12},{24,16},{28,20},{1,25},{... | collective-permute-start | bytes 1376264 | tf_op jit(solution)/shard_map/cond/branch_0_fun/ppermute | solution.py:481
  42.7 12.6 %collective-permute-start.7 = (bf16[1,128,1792]{2,1,0:T(8,128)(2,1)S(1)}, bf16[1,128,1792]{2,1,0:T(8,128)(2,1)S(1)}, u32[]{:S(2)}, u32[]{:S(2)}) collective-permute-start(bf16[1,128,1792]{2,1,0:T(8,128)(2,1)S(1)} %get-tuple-element.42), channel_id=1, source_target_pairs={{0,4},{4,0},{8,12},{12,8},{16,20},{20,16},{24,28},{28,24},{1,5},{5... | collective-permute-start | bytes 1376264 | tf_op jit(solution)/shard_map/cond/branch_0_fun/ppermute | solution.py:481

commit v2 on v1

--- a/solution.py
+++ b/solution.py
@@ -310,22 +310,26 @@
     by_place(third, me, plans(third, lengths_ref, rows, me), run)
 
 
-def group_parts(third, place, kinds, mine, messages):
+def group_parts(third, place, kinds, me, mine, message):
     size = kinds * GROUP
 
     def group(ref, number):
         return ref[number * size : (number + 1) * size, :]
 
-    own = [group(mine, 0), group(messages[0], 1)]
-    mate = [group(mine, 1), group(messages[0], 0)]
+    def sent(device, number):
+        return message[device, number * size : (number + 1) * size, :]
+
     if third is None:
-        return [own, mate]
-    _, near, far = messages
+        return [[group(mine, 0), group(message, 1)], [group(mine, 1), group(message, 0)]]
+    partner = me + 1 - 2 * lax.rem(me, 2)
+    own = [group(mine, 0), sent(partner, 1)]
+    mate = [group(mine, 1), sent(partner, 0)]
+    if place == "third":
+        return [own, mate, [group(mine, 2), sent(third + 1, 0), sent(third + 2, 1)]]
+    extra = sent(third, 2)
     if place == "even":
-        return [own + [group(near, 2)], mate]
-    if place == "odd":
-        return [own, mate + [group(far, 2)]]
-    return [own, mate, [group(mine, 2), group(near, 0), group(far, 1)]]
+        return [own + [jnp.where(me == third + 1, extra, 0.0)], mate]
+    return [own, mate + [jnp.where(me == third + 2, extra, 0.0)]]
 
 
 def merge_stats(scaling, parts):
@@ -376,15 +380,15 @@
 
 
 def values_kernel(third, heads, scaling, power, place_ref, lengths_ref, *refs):
-    count, messages = (2, 1) if third is None else (3, 3)
+    count = 2 if third is None else 3
     queries = [(refs[2 * n], refs[2 * n + 1]) for n in range(count)]
     refs = refs[2 * count :]
-    keys, mine, others = [(refs[0],), (refs[1],)], refs[2], refs[3 : 3 + messages]
-    value_own, value_back, shift_ref = refs[3 + messages :]
+    keys, mine, others = [(refs[0],), (refs[1],)], refs[2], refs[3]
+    value_own, value_back, shift_ref = refs[4:]
     rows, me, step = keys[0][0].shape[1], place_ref[0], pl.program_id(0)
 
     def run(place, plan):
-        groups = group_parts(third, place, 2, mine, others)
+        groups = group_parts(third, place, 2, me, mine, others)
         for number, parts in enumerate(groups):
             shift_ref[number * GROUP : (number + 1) * GROUP, :] = merge_stats(scaling, parts)
         out = Emitter({("v", 0): value_own, ("v", 1): value_back})
@@ -423,13 +427,12 @@
 
 def keys_kernel(third, heads, scaling, power, place_ref, lengths_ref, *refs):
     queries, keys, refs = split_refs(third, refs)
-    messages = 1 if third is None else 3
-    shift_ref, mine, others = refs[0], refs[1], refs[2 : 2 + messages]
-    key_own, key_back, *query_refs, total_ref = refs[2 + messages :]
+    shift_ref, mine, others = refs[:3]
+    key_own, key_back, *query_refs, total_ref = refs[3:]
     rows, me, step = keys[0][0].shape[1], place_ref[0], pl.program_id(0)
 
     def run(place, plan):
-        for number, parts in enumerate(group_parts(third, place, 1, mine, others)):
+        for number, parts in enumerate(group_parts(third, place, 1, me, mine, others)):
             total_ref[number * GROUP : (number + 1) * GROUP, :] = sum(parts)
         outs = {("k", 0): key_own, ("k", 1): key_back}
         outs.update({("q", slot): ref for slot, ref in enumerate(query_refs)})
@@ -472,22 +475,26 @@
     ring = third is None
     chain = [(s, s + 2) for s in devices if s + 2 < seq_size]
     ahead = [(s, (s + 2) % seq_size) for s in devices] if ring else chain
-    behind = [(s, (s - 2) % seq_size) for s in devices if ring or s >= 2]
+    behind = [(s, s - 2) for s in devices if s >= 2]
     if not ring:
         relay, to_even = [(third + 2, third)], [(third, third + 1)]
-        near, far = (to_even + [(third + 1, third)], relay + [(third, third + 2)])
 
     def send(value, pairs):
         return lax.ppermute(value, "seq", pairs)
 
     def exchange(value):
-        return [send(value, pairs) for pairs in ([mates] if ring else [mates, near, far])]
+        if ring:
+            return send(value, mates)
+        copies = jnp.broadcast_to(value[None], (seq_size, *value.shape))
+        return lax.all_to_all(copies, "seq", split_axis=0, concat_axis=0, tiled=True)
 
     smem = pl.BlockSpec(memory_space=pltpu.SMEM)
     wide = pl.BlockSpec((1, rows, part), lambda step: (0, 0, step))
     wide_shape = jax.ShapeDtypeStruct((1, rows, width), jnp.bfloat16)
 
-    def slim(kinds):
+    def slim(kinds, value=None):
+        if value is not None and value.ndim == 3:
+            return pl.BlockSpec((seq_size, count * kinds * GROUP, rows), lambda step: (0, 0, 0))
         return pl.BlockSpec((count * kinds * GROUP, rows), lambda step: (0, 0))
 
     def slim_shape(kinds):
@@ -500,7 +507,7 @@
             grid=(steps,),
             in_specs=[smem, smem]
             + [wide] * len(wides)
-            + [slim(kinds) for kinds, _ in slims]
+            + [slim(kinds, value) for kinds, value in slims]
             + [pl.BlockSpec(memory_space=pl.ANY)] * len(after),
             out_specs=[wide] * outs + [slim(kinds) for kinds in slim_outs],
             out_shape=[wide_shape] * outs + [slim_shape(kinds) for kinds in slim_outs],
@@ -527,7 +534,7 @@
     value_part, value_sent, shift = call(
         functools.partial(values_kernel, third, heads, scaling, power), 2,
         tensors[: 2 * count] + [key_vectors, key_back],
-        [(2, value) for value in [stats] + exchange(stats)], 2, [1],
+        [(2, stats), (2, exchange(stats))], 2, [1],
     )
     (dots,) = call(
         functools.partial(dots_kernel, third, heads, power), 2, tensors, [(1, shift)], 0, [1]
@@ -535,7 +542,7 @@
     value_received = send(value_sent, behind)
     key_part, key_sent, query_part, *query_sent = call(
         functools.partial(keys_kernel, third, heads, scaling, power), 4, tensors,
-        [(1, value) for value in [shift, dots] + exchange(dots)], 2 + count, [],
+        [(1, shift), (1, dots), (1, exchange(dots))], 2 + count, [],
         [pltpu.VMEM((count * GROUP, rows), jnp.float32)],
     )
     key_received = send(key_sent, behind)
@@ -555,7 +562,7 @@
             ),
         )(*flat)
 
-    (value_ready,) = total([[value_part, value_received]])
+    value_ready = (value_part.astype(jnp.float32) + value_received.astype(jnp.float32)).astype(jnp.bfloat16)
     key_ready, query_ready = total([[key_part, key_received], [query_part, *query_received]])
     return query_ready, key_ready, value_ready
 

time: 56.7 us -> 53.8 us (0.949)
  starting transfers between devices: 18.9 us -> 16.1 us
  Pallas kernels: 12.3 us -> 11.4 us
  other arithmetic: 0.75 us -> 1.65 us
    ppermute x9, starting transfers between devices: 18.9 us -> 16.1 us  [send(): return lax.ppermute(value, 'seq', pairs)]
    pallas_call x2 -> x1, Pallas kernels: 2.07 us -> 1.15 us  [total(): pl.pallas_call(functools.partial(sums_kernel, [len(terms) for terms in gr...]
    add x0 -> x1, other arithmetic: none -> 0.91 us  [halo_program(): value_part.astype(jnp.float32) + value_received.astype(jnp.float32)]
  transfers between devices with their start and end apart: 9 -> 9, of which waited for: 6 -> 6; matrix products, arithmetic and copies ran while one was open for 0% -> 2% of each run, Pallas kernels for 16% -> 19%
where the time goes in v2:
time: 53.8 us; the launch traced here: 53.6 us
  waiting for transfers between devices  22.4 us (42%)
  starting transfers between devices  16.1 us (30%)
  Pallas kernels  11.4 us (21%)
  other arithmetic  1.65 us (3%)
  between operations  1.29 us (2%)
  local copies, waits for them, and re-layouts  0.66 us (1%)
    ppermute x9, waiting for transfers between devices, send(): return lax.ppermute(value, 'seq', pairs)  22.4 us
    ppermute x9, starting transfers between devices, send(): return lax.ppermute(value, 'seq', pairs)  16.1 us
    pallas_call x4, Pallas kernels, call(): pl.pallas_call(kernel, grid=(steps,), in_specs=[smem, smem] + [wide] * le...  10.2 us
    pallas_call x1, Pallas kernels, total(): pl.pallas_call(functools.partial(sums_kernel, [len(terms) for terms in gr...  1.15 us
  transfers between devices with their start and end apart: 9, of which 6 were waited for; matrix products, arithmetic and copies ran while one was open for 2% of the time, Pallas kernels for 19%

profile of v2, /device:TPU:0, one launch (start us, length us, event | category | flops | bytes accessed | tf_op | source)
XLA Modules:
  0.0 53.6 jit_solution(13069823051156943200)
XLA Ops:
  0.6 0.6 %copy-done.10 = s32[8]{0:T(128)S(1)} copy-done((s32[8]{0:T(128)S(1)}, s32[8]{0:T(128)}, u32[]{:S(2)}) %copy-start.10) | copy-done | bytes 56
  1.3 0.7 %fusion = s32[]{:T(128)} fusion(s32[8]{0:T(128)S(1)} %copy-done.10, s32[1]{0:T(128)S(1)} %bitcast.10, s32[2]{0:T(128)S(1)} %bitcast.11, s32[3]{0:T(128)S(1)} %bitcast.12, s32[4]{0:T(128)S(1)} %bitcast.13, s32[5]{0:T(128)S(1)} %bitcast.14, s32[6]{0:T(128)S(1)} %bitcast.15, s32[7]{0:T(128)S(1)} %bitcast.16), kind=kLoop, calls=%fused_computation.4 | loop fusion | flops 159 | bytes 148 | tf_op jit(solution)/shard_map/reduce_sum | solution.py:576
  2.7 50.9 %conditional.4 = (bf16[1,128,1792]{2,1,0:T(8,128)(2,1)}, bf16[1,128,1792]{2,1,0:T(8,128)(2,1)}, bf16[1,128,1792]{2,1,0:T(8,128)(2,1)}) conditional(s32[]{:T(128)} %clamp.3, (bf16[1,128,1792]{2,1,0:T(8,128)(2,1)}, bf16[1,128,1792]{2,1,0:T(8,128)(2,1)}, s32[8]{0:T(128)S(1)}, bf16[1,128,1792]{2,1,0:T(8,128)(2,1)}, ...), branch_computations={%region_1.2_spmd, %region_2.3_spmd, %region_3.4_spmd} | conditional | flops 3172040704 | bytes 48370264
  2.7 3.0 %collective-permute-start = (bf16[1,128,1792]{2,1,0:T(8,128)(2,1)}, bf16[1,128,1792]{2,1,0:T(8,128)(2,1)S(1)}, u32[]{:S(2)}, u32[]{:S(2)}) collective-permute-start(bf16[1,128,1792]{2,1,0:T(8,128)(2,1)} %get-tuple-element.41.refs_0_), channel_id=1, source_target_pairs={{0,4},{4,0},{8,12},{12,8},{16,20},{20,16},{24,28},{28,24},{1,5},{5... | collective-permute-start | bytes 1376264 | tf_op jit(solution)/shard_map/cond/branch_0_fun/ppermute | solution.py:483
  5.7 3.5 %collective-permute-start.1 = (bf16[1,128,1792]{2,1,0:T(8,128)(2,1)}, bf16[1,128,1792]{2,1,0:T(8,128)(2,1)S(1)}, u32[]{:S(2)}, u32[]{:S(2)}) collective-permute-start(bf16[1,128,1792]{2,1,0:T(8,128)(2,1)} %get-tuple-element.42.refs_2_.refs_4_), channel_id=1, source_target_pairs={{0,8},{4,12},{8,16},{12,20},{16,24},{20,28},{1,9},{5,13},{9,17},{1... | collective-permute-start | bytes 1376264 | tf_op jit(solution)/shard_map/cond/branch_0_fun/ppermute | solution.py:483
  9.2 0.6 %collective-permute-start.2 = (bf16[1,128,1792]{2,1,0:T(8,128)(2,1)}, bf16[1,128,1792]{2,1,0:T(8,128)(2,1)S(1)}, u32[]{:S(2)}, u32[]{:S(2)}) collective-permute-start(bf16[1,128,1792]{2,1,0:T(8,128)(2,1)} %get-tuple-element.43.refs_4_), channel_id=1, source_target_pairs={{0,4},{4,0},{8,12},{12,8},{16,20},{20,16},{24,28},{28,24},{1,5},{5... | collective-permute-start | bytes 1376264 | tf_op jit(solution)/shard_map/cond/branch_0_fun/ppermute | solution.py:483
  9.8 1.6 %collective-permute-start.3 = (bf16[1,128,1792]{2,1,0:T(8,128)(2,1)}, bf16[1,128,1792]{2,1,0:T(8,128)(2,1)S(1)}, u32[]{:S(2)}, u32[]{:S(2)}) collective-permute-start(bf16[1,128,1792]{2,1,0:T(8,128)(2,1)} %get-tuple-element.44.refs_5_), channel_id=1, source_target_pairs={{0,8},{4,12},{8,16},{12,20},{16,24},{20,28},{24,0},{28,4},{1,9},{5... | collective-permute-start | bytes 1376264 | tf_op jit(solution)/shard_map/cond/branch_0_fun/ppermute | solution.py:483
  11.4 5.9 %collective-permute-done.refs_1_.refs_2_ = bf16[1,128,1792]{2,1,0:T(8,128)(2,1)S(1)} collective-permute-done((bf16[1,128,1792]{2,1,0:T(8,128)(2,1)}, bf16[1,128,1792]{2,1,0:T(8,128)(2,1)S(1)}, u32[]{:S(2)}, u32[]{:S(2)}) %collective-permute-start) | collective-permute-done | bytes 458784 | tf_op jit(solution)/shard_map/cond/branch_0_fun/ppermute | solution.py:483
  17.3 3.2 %collective-permute-done.1.refs_3_.refs_5_.refs_6_ = bf16[1,128,1792]{2,1,0:T(8,128)(2,1)S(1)} collective-permute-done((bf16[1,128,1792]{2,1,0:T(8,128)(2,1)}, bf16[1,128,1792]{2,1,0:T(8,128)(2,1)S(1)}, u32[]{:S(2)}, u32[]{:S(2)}) %collective-permute-start.1) | collective-permute-done | bytes 458784 | tf_op jit(solution)/shard_map/cond/branch_0_fun/ppermute | solution.py:483
  20.4 2.6 %branch_0_fun.5 = (bf16[1,128,1792]{2,1,0:T(8,128)(2,1)S(1)}, bf16[1,128,1792]{2,1,0:T(8,128)(2,1)S(1)}, f32[32,128]{1,0:T(8,128)S(1)}) custom-call(s32[1]{0:T(128)} %bitcast.place_ref, s32[8]{0:T(128)S(1)} %get-tuple-element.40.lengths_ref, bf16[1,128,1792]{2,1,0:T(8,128)(2,1)} %get-tuple-element.41.refs_0_, ...), custom_call_target="tpu_custom_call" | custom-call | flops 352321536 | bytes 4587520 | tf_op jit(solution)/shard_map/cond/branch_0_fun/pallas_call | solution.py:505
  23.1 0.6 %collective-permute-start.4 = (f32[32,128]{1,0:T(8,128)S(1)}, f32[32,128]{1,0:T(8,128)S(1)}, u32[]{:S(2)}, u32[]{:S(2)}) collective-permute-start(f32[32,128]{1,0:T(8,128)S(1)} %get-tuple-element.47.refs_6_), channel_id=1, source_target_pairs={{0,4},{4,0},{8,12},{12,8},{16,20},{20,16},{24,28},{28,24},{1,5},{5... | collective-permute-start | bytes 49160 | tf_op jit(solution)/shard_map/cond/branch_0_fun/ppermute | solution.py:483
  23.7 2.8 %collective-permute-done.2.refs_3_ = bf16[1,128,1792]{2,1,0:T(8,128)(2,1)S(1)} collective-permute-done((bf16[1,128,1792]{2,1,0:T(8,128)(2,1)}, bf16[1,128,1792]{2,1,0:T(8,128)(2,1)S(1)}, u32[]{:S(2)}, u32[]{:S(2)}) %collective-permute-start.2) | collective-permute-done | bytes 458784 | tf_op jit(solution)/shard_map/cond/branch_0_fun/ppermute | solution.py:483
  26.4 0.4 collective-permute-done.4.refs_7_
  26.9 2.3 %branch_0_fun.6 = (bf16[1,128,1792]{2,1,0:T(8,128)(2,1)S(1)}, bf16[1,128,1792]{2,1,0:T(8,128)(2,1)S(1)}, f32[16,128]{1,0:T(8,128)S(1)}) custom-call(s32[1]{0:T(128)} %bitcast.place_ref, s32[8]{0:T(128)S(1)} %get-tuple-element.40.lengths_ref, bf16[1,128,1792]{2,1,0:T(8,128)(2,1)S(1)} %copy-done.4, bf16[1,128,1792]{2,1,0:T(8,128)(2,1)S(1)} %get-tuple-element.45.refs_1_, ...), custom_call_target="tpu_custom_call" | custom-call | flops 704643072 | bytes 4587520 | tf_op jit(solution)/shard_map/cond/branch_0_fun/pallas_call | solution.py:505
  29.2 1.3 %collective-permute-start.8 = (bf16[1,128,1792]{2,1,0:T(8,128)(2,1)S(1)}, bf16[1,128,1792]{2,1,0:T(8,128)(2,1)S(1)}, u32[]{:S(2)}, u32[]{:S(2)}) collective-permute-start(bf16[1,128,1792]{2,1,0:T(8,128)(2,1)S(1)} %get-tuple-element.56), channel_id=1, source_target_pairs={{8,0},{12,4},{16,8},{20,12},{24,16},{28,20},{9,1},{13,5},{17,9},{2... | collective-permute-start | bytes 1376264 | tf_op jit(solution)/shard_map/cond/branch_0_fun/ppermute | solution.py:483
  30.5 2.1 %branch_0_fun.7.refs_9_ = f32[16,128]{1,0:T(8,128)S(1)} custom-call(s32[1]{0:T(128)} %bitcast.place_ref, s32[8]{0:T(128)S(1)} %get-tuple-element.40.lengths_ref, bf16[1,128,1792]{2,1,0:T(8,128)(2,1)S(1)} %copy-done.4, bf16[1,128,1792]{2,1,0:T(8,128)(2,1)S(1)} %get-tuple-element.45.refs_1_, bf16[1,128,1792]{2,1,0:T(8,128)(2,1)S(1)} %collective-permute-done.refs_1_.refs_2_, ...), custom_call_target="tpu_custom_call" | custom-call | flops 704643072 | bytes 4587520 | tf_op jit(solution)/shard_map/cond/branch_0_fun/pallas_call | solution.py:505
  32.6 1.9 %collective-permute-start.5 = (f32[16,128]{1,0:T(8,128)S(1)}, f32[16,128]{1,0:T(8,128)S(1)}, u32[]{:S(2)}, u32[]{:S(2)}) collective-permute-start(f32[16,128]{1,0:T(8,128)S(1)} %branch_0_fun.7.refs_9_), channel_id=1, source_target_pairs={{0,4},{4,0},{8,12},{12,8},{16,20},{20,16},{24,28},{28,24},{1,5},{5... | collective-permute-start | bytes 24584 | tf_op jit(solution)/shard_map/cond/branch_0_fun/ppermute | solution.py:483
  34.6 1.8 %collective-permute-done.5.refs_10_ = f32[16,128]{1,0:T(8,128)S(1)} collective-permute-done((f32[16,128]{1,0:T(8,128)S(1)}, f32[16,128]{1,0:T(8,128)S(1)}, u32[]{:S(2)}, u32[]{:S(2)}) %collective-permute-start.5) | collective-permute-done | bytes 8224 | tf_op jit(solution)/shard_map/cond/branch_0_fun/ppermute | solution.py:483
  36.3 3.2 %branch_0_fun.8 = (bf16[1,128,1792]{2,1,0:T(8,128)(2,1)S(1)}, bf16[1,128,1792]{2,1,0:T(8,128)(2,1)S(1)}, bf16[1,128,1792]{2,1,0:T(8,128)(2,1)S(1)}, bf16[1,128,1792]{2,1,0:T(8,128)(2,1)S(1)}) custom-call(s32[1]{0:T(128)} %bitcast.place_ref, s32[8]{0:T(128)S(1)} %get-tuple-element.40.lengths_ref, bf16[1,128,1792]{2,1,0:T(8,128)(2,1)S(1)} %copy-done.4, ...), custom_call_target="tpu_custom_call" | custom-call | flops 1409286144 | bytes 4587520 | tf_op jit(solution)/shard_map/cond/branch_0_fun/pallas_call | solution.py:505
  39.5 1.3 %collective-permute-start.6 = (bf16[1,128,1792]{2,1,0:T(8,128)(2,1)S(1)}, bf16[1,128,1792]{2,1,0:T(8,128)(2,1)S(1)}, u32[]{:S(2)}, u32[]{:S(2)}) collective-permute-start(bf16[1,128,1792]{2,1,0:T(8,128)(2,1)S(1)} %get-tuple-element.50), channel_id=1, source_target_pairs={{8,0},{12,4},{16,8},{20,12},{24,16},{28,20},{9,1},{13,5},{17,9},{2... | collective-permute-start | bytes 1376264 | tf_op jit(solution)/shard_map/cond/branch_0_fun/ppermute | solution.py:483
  40.8 2.3 %collective-permute-start.7 = (bf16[1,128,1792]{2,1,0:T(8,128)(2,1)S(1)}, bf16[1,128,1792]{2,1,0:T(8,128)(2,1)S(1)}, u32[]{:S(2)}, u32[]{:S(2)}) collective-permute-start(bf16[1,128,1792]{2,1,0:T(8,128)(2,1)S(1)} %get-tuple-element.52), channel_id=1, source_target_pairs={{0,4},{4,0},{8,12},{12,8},{16,20},{20,16},{24,28},{28,24},{1,5},{5... | collective-permute-start | bytes 1376264 | tf_op jit(solution)/shard_map/cond/branch_0_fun/ppermute | solution.py:483
  43.2 0.9 %convert_add_fusion = bf16[1,128,1792]{2,1,0:T(8,128)(2,1)} fusion(bf16[1,128,1792]{2,1,0:T(8,128)(2,1)S(1)} %collective-permute-done.8, bf16[1,128,1792]{2,1,0:T(8,128)(2,1)S(1)} %get-tuple-element.55), kind=kLoop, calls=%fused_computation | loop fusion | flops 917504 | bytes 1376256 | tf_op jit(solution)/shard_map/cond/branch_0_fun/add | solution.py:565
  44.1 8.3 %collective-permute-done.6.refs_1_ = bf16[1,128,1792]{2,1,0:T(8,128)(2,1)S(1)} collective-permute-done((bf16[1,128,1792]{2,1,0:T(8,128)(2,1)S(1)}, bf16[1,128,1792]{2,1,0:T(8,128)(2,1)S(1)}, u32[]{:S(2)}, u32[]{:S(2)}) %collective-permute-start.6) | collective-permute-done | bytes 458784 | tf_op jit(solution)/shard_map/cond/branch_0_fun/ppermute | solution.py:483
  52.4 1.2 %branch_0_fun.9 = (bf16[1,128,1792]{2,1,0:T(8,128)(2,1)}, bf16[1,128,1792]{2,1,0:T(8,128)(2,1)}) custom-call(bf16[1,128,1792]{2,1,0:T(8,128)(2,1)S(1)} %get-tuple-element.49.refs_0_, bf16[1,128,1792]{2,1,0:T(8,128)(2,1)S(1)} %collective-permute-done.6.refs_1_, bf16[1,128,1792]{2,1,0:T(8,128)(2,1)S(1)} %get-tuple-element.51.refs_2_, ...), custom_call_target="tpu_custom_call" | custom-call | flops 229376 | bytes 1835008 | tf_op jit(solution)/shard_map/cond/branch_0_fun/pallas_call | solution.py:553
  (8 shorter events, 0.0 us)
Async XLA Ops:
  0.6 0.7 %copy-start.10 = (s32[8]{0:T(128)S(1)}, s32[8]{0:T(128)}, u32[]{:S(2)}) copy-start(s32[8]{0:T(128)} %param.12) | copy-start | bytes 100
  2.7 14.6 %collective-permute-start = (bf16[1,128,1792]{2,1,0:T(8,128)(2,1)}, bf16[1,128,1792]{2,1,0:T(8,128)(2,1)S(1)}, u32[]{:S(2)}, u32[]{:S(2)}) collective-permute-start(bf16[1,128,1792]{2,1,0:T(8,128)(2,1)} %get-tuple-element.41.refs_0_), channel_id=1, source_target_pairs={{0,4},{4,0},{8,12},{12,8},{16,20},{20,16},{24,28},{28,24},{1,5},{5... | collective-permute-start | bytes 1376264 | tf_op jit(solution)/shard_map/cond/branch_0_fun/ppermute | solution.py:483
  5.7 14.7 %collective-permute-start.1 = (bf16[1,128,1792]{2,1,0:T(8,128)(2,1)}, bf16[1,128,1792]{2,1,0:T(8,128)(2,1)S(1)}, u32[]{:S(2)}, u32[]{:S(2)}) collective-permute-start(bf16[1,128,1792]{2,1,0:T(8,128)(2,1)} %get-tuple-element.42.refs_2_.refs_4_), channel_id=1, source_target_pairs={{0,8},{4,12},{8,16},{12,20},{16,24},{20,28},{1,9},{5,13},{9,17},{1... | collective-permute-start | bytes 1376264 | tf_op jit(solution)/shard_map/cond/branch_0_fun/ppermute | solution.py:483
  9.2 17.2 %collective-permute-start.2 = (bf16[1,128,1792]{2,1,0:T(8,128)(2,1)}, bf16[1,128,1792]{2,1,0:T(8,128)(2,1)S(1)}, u32[]{:S(2)}, u32[]{:S(2)}) collective-permute-start(bf16[1,128,1792]{2,1,0:T(8,128)(2,1)} %get-tuple-element.43.refs_4_), channel_id=1, source_target_pairs={{0,4},{4,0},{8,12},{12,8},{16,20},{20,16},{24,28},{28,24},{1,5},{5... | collective-permute-start | bytes 1376264 | tf_op jit(solution)/shard_map/cond/branch_0_fun/ppermute | solution.py:483
  9.8 20.7 %collective-permute-start.3 = (bf16[1,128,1792]{2,1,0:T(8,128)(2,1)}, bf16[1,128,1792]{2,1,0:T(8,128)(2,1)S(1)}, u32[]{:S(2)}, u32[]{:S(2)}) collective-permute-start(bf16[1,128,1792]{2,1,0:T(8,128)(2,1)} %get-tuple-element.44.refs_5_), channel_id=1, source_target_pairs={{0,8},{4,12},{8,16},{12,20},{16,24},{20,28},{24,0},{28,4},{1,9},{5... | collective-permute-start | bytes 1376264 | tf_op jit(solution)/shard_map/cond/branch_0_fun/ppermute | solution.py:483
  20.4 6.5 %copy-start.4 = (bf16[1,128,1792]{2,1,0:T(8,128)(2,1)S(1)}, bf16[1,128,1792]{2,1,0:T(8,128)(2,1)}, u32[]{:S(2)}) copy-start(bf16[1,128,1792]{2,1,0:T(8,128)(2,1)} %get-tuple-element.41.refs_0_) | copy-start | bytes 1376260
  20.4 6.5 %copy-start.7 = (bf16[1,128,1792]{2,1,0:T(8,128)(2,1)S(1)}, bf16[1,128,1792]{2,1,0:T(8,128)(2,1)}, u32[]{:S(2)}) copy-start(bf16[1,128,1792]{2,1,0:T(8,128)(2,1)} %get-tuple-element.42.refs_2_.refs_4_) | copy-start | bytes 1376260
  23.1 3.8 %collective-permute-start.4 = (f32[32,128]{1,0:T(8,128)S(1)}, f32[32,128]{1,0:T(8,128)S(1)}, u32[]{:S(2)}, u32[]{:S(2)}) collective-permute-start(f32[32,128]{1,0:T(8,128)S(1)} %get-tuple-element.47.refs_6_), channel_id=1, source_target_pairs={{0,4},{4,0},{8,12},{12,8},{16,20},{20,16},{24,28},{28,24},{1,5},{5... | collective-permute-start | bytes 49160 | tf_op jit(solution)/shard_map/cond/branch_0_fun/ppermute | solution.py:483
  29.2 14.0 %collective-permute-start.8 = (bf16[1,128,1792]{2,1,0:T(8,128)(2,1)S(1)}, bf16[1,128,1792]{2,1,0:T(8,128)(2,1)S(1)}, u32[]{:S(2)}, u32[]{:S(2)}) collective-permute-start(bf16[1,128,1792]{2,1,0:T(8,128)(2,1)S(1)} %get-tuple-element.56), channel_id=1, source_target_pairs={{8,0},{12,4},{16,8},{20,12},{24,16},{28,20},{9,1},{13,5},{17,9},{2... | collective-permute-start | bytes 1376264 | tf_op jit(solution)/shard_map/cond/branch_0_fun/ppermute | solution.py:483
  32.6 3.7 %collective-permute-start.5 = (f32[16,128]{1,0:T(8,128)S(1)}, f32[16,128]{1,0:T(8,128)S(1)}, u32[]{:S(2)}, u32[]{:S(2)}) collective-permute-start(f32[16,128]{1,0:T(8,128)S(1)} %branch_0_fun.7.refs_9_), channel_id=1, source_target_pairs={{0,4},{4,0},{8,12},{12,8},{16,20},{20,16},{24,28},{28,24},{1,5},{5... | collective-permute-start | bytes 24584 | tf_op jit(solution)/shard_map/cond/branch_0_fun/ppermute | solution.py:483
  39.5 12.9 %collective-permute-start.6 = (bf16[1,128,1792]{2,1,0:T(8,128)(2,1)S(1)}, bf16[1,128,1792]{2,1,0:T(8,128)(2,1)S(1)}, u32[]{:S(2)}, u32[]{:S(2)}) collective-permute-start(bf16[1,128,1792]{2,1,0:T(8,128)(2,1)S(1)} %get-tuple-element.50), channel_id=1, source_target_pairs={{8,0},{12,4},{16,8},{20,12},{24,16},{28,20},{9,1},{13,5},{17,9},{2... | collective-permute-start | bytes 1376264 | tf_op jit(solution)/shard_map/cond/branch_0_fun/ppermute | solution.py:483
  40.8 11.6 %collective-permute-start.7 = (bf16[1,128,1792]{2,1,0:T(8,128)(2,1)S(1)}, bf16[1,128,1792]{2,1,0:T(8,128)(2,1)S(1)}, u32[]{:S(2)}, u32[]{:S(2)}) collective-permute-start(bf16[1,128,1792]{2,1,0:T(8,128)(2,1)S(1)} %get-tuple-element.52), channel_id=1, source_target_pairs={{0,4},{4,0},{8,12},{12,8},{16,20},{20,16},{24,28},{28,24},{1,5},{5... | collective-permute-start | bytes 1376264 | tf_op jit(solution)/shard_map/cond/branch_0_fun/ppermute | solution.py:483
